TPU v7x, 512 devices: a whole 4x4x16 slice. The times are simulated.
512 devices in a mesh: blk: 32 (over z_hi, x, core), head: 16 (over y, z_lo).
Axes of the slice: x: 4, y: 4, z: 16 (z_hi: 4, z_lo: 4; z = z_hi * 4 + z_lo), core: 2. Of those that a mesh axis runs over, the one named last changes fastest.
Arguments:
- query: bfloat16 [4096, 128, 128], P(('blk', 'head')), may hold values from -24 to 24
- key: bfloat16 [4096, 8, 128], P(('blk', 'head')), may hold values from -18 to 18
- value: bfloat16 [4096, 8, 128], P(('blk', 'head')), may hold values from -6 to 6
- out_grad: bfloat16 [4096, 128, 128], P(('blk', 'head')), may hold values from -6 to 6
- block_order: int32 [64], replicated, may hold values from 0 to 63, each once
Outputs:
- query_grad: bfloat16 [4096, 128, 128], P(('blk', 'head'))
- key_grad: bfloat16 [4096, 8, 128], P(('blk', 'head'))
- value_grad: bfloat16 [4096, 8, 128], P(('blk', 'head'))
Inputs may be any that keep to these rules, and one draw needn't show every extreme that they name: `block_order`: each value appears once.
All inputs are finite; a program needn't handle non-finite values.
Results may differ from a plain program's by a relative error of at most 0.012.
Values may be sent and summed in bfloat16 or wider, within the bound.
A program may use at most 64 MiB of HBM per device.

v0:
```python
import math

import jax
import jax.numpy as jnp
from jax import lax
from jax.sharding import PartitionSpec as P


def lookup(table, index):
    entries = table.shape[0]
    hits = index[:, None] == jnp.arange(entries, dtype=jnp.int32)[None, :]
    return jnp.sum(jnp.where(hits, table[None, :], 0), axis=1)


def scored(queries, key_blk, query_pos, pos_blk, score_scale):
    logits = (
        jnp.einsum("qkgd,tkd->kgqt", queries, key_blk, preferred_element_type=jnp.float32)
        * score_scale
    )
    allowed = pos_blk[None, None, None, :] <= query_pos[None, None, :, None]
    return (logits, allowed)


def on_device(query, key, value, out_grad, block_order):
    head_count = lax.axis_size("head")
    tokens_here = query.shape[0]
    head_width = query.shape[2]
    kv_heads = key.shape[1]
    repeat = max(1, head_count // kv_heads)
    key_rep = jnp.repeat(key, repeat, axis=1)
    value_rep = jnp.repeat(value, repeat, axis=1)
    q_local, g_local, k_local, v_local = (
        lax.all_to_all(query, "head", split_axis=1, concat_axis=0, tiled=True),
        lax.all_to_all(out_grad, "head", split_axis=1, concat_axis=0, tiled=True),
        lax.all_to_all(key_rep, "head", split_axis=1, concat_axis=0, tiled=True),
        lax.all_to_all(value_rep, "head", split_axis=1, concat_axis=0, tiled=True),
    )
    row_count = q_local.shape[0]
    local_heads = q_local.shape[1]
    local_kv = k_local.shape[1]
    group_size = local_heads // local_kv
    queries = q_local.reshape(row_count, local_kv, group_size, head_width)
    grads_out = g_local.reshape(row_count, local_kv, group_size, head_width)
    k_all, v_all = (
        lax.all_gather(k_local, "blk", axis=0, tiled=True),
        lax.all_gather(v_local, "blk", axis=0, tiled=True),
    )
    seq_len = k_all.shape[0]
    piece_len = row_count // 2
    piece_count = seq_len // piece_len
    block_len = math.gcd(seq_len, 512)
    score_scale = head_width ** (-0.5)
    slots = jnp.arange(seq_len, dtype=jnp.int32)
    key_pos = lookup(block_order, slots // piece_len) * piece_len + slots % piece_len
    query_pos = lax.dynamic_slice_in_dim(key_pos, lax.axis_index("blk") * row_count, row_count, 0)
    last_pos = jnp.max(query_pos)
    owners = jnp.arange(piece_count, dtype=jnp.int32)
    inverse = jnp.sum(
        jnp.where(block_order[None, :] == owners[:, None], owners[None, :], 0), axis=1
    )
    k_loop = k_all.reshape(piece_count, piece_len, local_kv, head_width)[inverse].reshape(
        seq_len, local_kv, head_width
    )
    v_loop = v_all.reshape(piece_count, piece_len, local_kv, head_width)[inverse].reshape(
        seq_len, local_kv, head_width
    )
    step_count = last_pos // block_len + 1

    def take_block(step_index):
        offset = step_index * block_len
        key_blk = lax.dynamic_slice_in_dim(k_loop, offset, block_len, 0)
        value_blk = lax.dynamic_slice_in_dim(v_loop, offset, block_len, 0)
        pos_blk = lax.dynamic_slice_in_dim(slots, offset, block_len, 0)
        return (key_blk, value_blk, pos_blk)

    def norm_step(step_index, carry):
        running_max, exp_sum = carry
        key_blk, value_blk, pos_blk = take_block(step_index)
        logits, allowed = scored(queries, key_blk, query_pos, pos_blk, score_scale)
        masked = jnp.where(allowed, logits, -jnp.inf)
        new_max = jnp.maximum(running_max, jnp.max(masked, axis=-1))
        exp_sum = exp_sum * jnp.exp(running_max - new_max) + jnp.sum(
            jnp.exp(masked - new_max[..., None]), axis=-1
        )
        return (new_max, exp_sum)

    stat_shape = (local_kv, group_size, row_count)
    running_max, exp_sum = lax.fori_loop(
        0,
        step_count,
        norm_step,
        (jnp.full(stat_shape, -1e30, jnp.float32), jnp.zeros(stat_shape, jnp.float32)),
    )
    log_norm = running_max + jnp.log(exp_sum)

    def output_step(step_index, out_acc):
        key_blk, value_blk, pos_blk = take_block(step_index)
        logits, allowed = scored(queries, key_blk, query_pos, pos_blk, score_scale)
        probs_low = jnp.where(allowed, jnp.exp(logits - log_norm[..., None]), 0.0).astype(
            jnp.bfloat16
        )
        return out_acc + jnp.einsum(
            "kgqt,tkd->kgqd", probs_low, value_blk, preferred_element_type=jnp.float32
        )

    attn_out = lax.fori_loop(
        0,
        step_count,
        output_step,
        jnp.zeros((local_kv, group_size, row_count, head_width), jnp.float32),
    )
    delta = jnp.sum(jnp.transpose(grads_out, (1, 2, 0, 3)).astype(jnp.float32) * attn_out, axis=-1)

    def tile_terms(key_blk, value_blk, pos_blk):
        logits, allowed = scored(queries, key_blk, query_pos, pos_blk, score_scale)
        probs = jnp.where(allowed, jnp.exp(logits - log_norm[..., None]), 0.0)
        probs_low = probs.astype(jnp.bfloat16)
        dprobs = jnp.einsum(
            "qkgd,tkd->kgqt", grads_out, value_blk, preferred_element_type=jnp.float32
        )
        dscores = (probs * (dprobs - delta[..., None])).astype(jnp.bfloat16)
        dq_part = jnp.einsum("kgqt,tkd->qkgd", dscores, key_blk, preferred_element_type=jnp.float32)
        dk_part = (
            jnp.einsum("kgqt,qkgd->tkd", dscores, queries, preferred_element_type=jnp.float32)
            * score_scale
        )
        dv_part = jnp.einsum(
            "kgqt,qkgd->tkd", probs_low, grads_out, preferred_element_type=jnp.float32
        )
        return (dq_part, dk_part, dv_part)

    dq_zero = jnp.zeros((row_count, local_kv, group_size, head_width), jnp.float32)

    def grad_step(step_index, carry):
        dq_acc, dk_term, dv_term = carry
        key_blk, value_blk, pos_blk = take_block(step_index)
        dq_part, dk_part, dv_part = tile_terms(key_blk, value_blk, pos_blk)
        offset = step_index * block_len
        dk_term = lax.dynamic_update_slice_in_dim(dk_term, dk_part, offset, 0)
        dv_term = lax.dynamic_update_slice_in_dim(dv_term, dv_part, offset, 0)
        return (dq_acc + dq_part, dk_term, dv_term)

    term_zero = jnp.zeros((seq_len, local_kv, head_width), jnp.float32)
    dq_acc, dk_term, dv_term = lax.fori_loop(
        0, step_count, grad_step, (dq_zero, term_zero, term_zero)
    )
    dk_term = dk_term.reshape(piece_count, piece_len, local_kv, head_width)[block_order].reshape(
        seq_len, local_kv, head_width
    )
    dv_term = dv_term.reshape(piece_count, piece_len, local_kv, head_width)[block_order].reshape(
        seq_len, local_kv, head_width
    )
    dk_mine, dv_mine = (
        lax.psum_scatter(dk_term, "blk", scatter_dimension=0, tiled=True),
        lax.psum_scatter(dv_term, "blk", scatter_dimension=0, tiled=True),
    )
    key_mine = jnp.stack((dk_mine, dv_mine), axis=2)
    dq_low = (dq_acc * score_scale).astype(jnp.bfloat16).reshape(row_count, local_heads, head_width)
    dq_home = lax.all_to_all(dq_low, "head", split_axis=0, concat_axis=1, tiled=True)
    kv_wide = lax.all_to_all(
        key_mine.astype(jnp.bfloat16), "head", split_axis=0, concat_axis=1, tiled=True
    ).astype(key_mine.dtype)
    kv_home = jnp.sum(kv_wide.reshape(tokens_here, kv_heads, repeat, 2, head_width), axis=2).astype(
        jnp.bfloat16
    )
    return (dq_home, kv_home[:, :, 0], kv_home[:, :, 1])


def solution(mesh):
    in_specs = (
        P(("blk", "head"), None, None),
        P(("blk", "head"), None, None),
        P(("blk", "head"), None, None),
        P(("blk", "head"), None, None),
        P(),
    )
    out_specs = (
        P(("blk", "head"), None, None),
        P(("blk", "head"), None, None),
        P(("blk", "head"), None, None),
    )
    return jax.shard_map(
        on_device, mesh=mesh, in_specs=in_specs, out_specs=out_specs, check_vma=False
    )
```

profile of v0, /device:TPU:1, one launch (start us, length us, event | category | flops | bytes accessed | tf_op | source)
XLA Modules:
  0.0 497.6 jit_solution(9026350387373698722)
XLA Ops:
  8.5 9.2 %all-to-all-start = ((bf16[8,16,128]{2,0,1:T(8,128)(2,1)}), bf16[8,16,128]{2,0,1:T(8,128)(2,1)S(1)}, u32[]{:S(2)}, u32[]{:S(2)}) async-start(bf16[8,16,128]{2,0,1:T(8,128)(2,1)} %bitcast.43), calls=%async_computation | async-start | bytes 65536 | tf_op jit(solution)/shard_map/all_to_all | solution.py:35
  18.4 6.1 %all-to-all-done = bf16[8,16,128]{2,0,1:T(8,128)(2,1)S(1)} async-done(((bf16[8,16,128]{2,0,1:T(8,128)(2,1)}), bf16[8,16,128]{2,0,1:T(8,128)(2,1)S(1)}, u32[]{:S(2)}, u32[]{:S(2)}) %all-to-all-start) | async-done | bytes 32800 | tf_op jit(solution)/shard_map/all_to_all | solution.py:35
  25.2 3.5 all-to-all-start.2
  29.5 1.8 copy.64
  31.3 4.2 all-to-all-done.2
  35.5 3.5 all-to-all-start.1
  39.1 1.8 copy.67
  41.8 5.2 %all-to-all-done.1 = bf16[8,128,128]{2,0,1:T(8,128)(2,1)S(1)} async-done(((bf16[8,128,128]{2,0,1:T(8,128)(2,1)}), bf16[8,128,128]{2,0,1:T(8,128)(2,1)S(1)}, u32[]{:S(2)}, u32[]{:S(2)}) %all-to-all-start.1) | async-done | bytes 262176 | tf_op jit(solution)/shard_map/all_to_all | solution.py:33
  47.0 3.5 all-to-all-start.3
  54.3 4.3 all-to-all-done.3
  58.6 50.1 %all-gather.3.cloned.1.call-done = bf16[4096,1,128]{2,0,1:T(8,128)(2,1)} async-done(((bf16[128,1,128]{2,0,1:T(8,128)(2,1)}), bf16[4096,1,128]{2,0,1:T(8,128)(2,1)}) %all-gather.3.cloned.1.call-update) | async-done | bytes 1048592 | tf_op jit(solution)/shard_map/all_gather | solution.py:45
  108.7 2.0 gather_fusion
  110.7 7.1 %while.36 = (s32[]{:T(128)}, f32[1,8,128]{2,1,0:T(8,128)S(1)}, f32[1,8,128]{2,1,0:T(8,128)S(1)}, s32[]{:T(128)}, s32[4096]{0:T(1024)S(1)}, /*index=5*/s32[128]{0...) while((s32[]{:T(128)}, f32[1,8,128]{2,1,0:T(8,128)S(1)}, ...), condition=%wide.region_6.7_spmd, body=%wide.region_3.6_spmd.sunk | while | flops 137955328 | bytes 4844203 | solution.py:88
  117.8 59.5 %all-gather.5.cloned.1.call-done = bf16[4096,1,128]{2,0,1:T(8,128)(2,1)} async-done(((bf16[128,1,128]{2,0,1:T(8,128)(2,1)}), bf16[4096,1,128]{2,0,1:T(8,128)(2,1)}) %all-gather.5.cloned.1.call-update) | async-done | bytes 1048592 | tf_op jit(solution)/shard_map/all_gather | solution.py:46
  177.3 2.0 gather_fusion.1
  179.4 7.6 %while.37 = (s32[]{:T(128)}, f32[1,8,128,128]{3,2,1,0:T(8,128)S(1)}, s32[]{:T(128)}, s32[4096]{0:T(1024)S(1)}, s32[128]{0:T(128)S(1)}, /*index=5*/bf16[4096,1,12...) while((s32[]{:T(128)}, ...), condition=%wide.region_8.9_spmd, body=%wide.region_7.8_spmd.sunk | while | flops 270729216 | bytes 1715887 | solution.py:106
  190.0 35.6 %while.38 = (s32[]{:T(128)}, f32[128,1,8,128]{0,3,2,1:T(8,128)S(1)}, f32[4096,1,128]{2,0,1:T(8,128)S(1)}, f32[4096,1,128]{2,0,1:T(8,128)}, s32[]{:T(128)}, /*ind...) while((s32[]{:T(128)}, ...), condition=%wide.region_11.12_spmd, body=%wide.region_10.11_spmd.sunk | while | flops 675020800 | bytes 12597987 | solution.py:144
  225.6 3.6 gather_fusion.3
  229.3 2.0 gather_fusion.2
  232.3 4.5 all-to-all-start.4
  236.8 120.5 %reduce-scatter.5.cloned.1.call-done = f32[128,1,128]{2,0,1:T(8,128)} async-done(((f32[4096,1,128]{2,0,1:T(8,128)}), f32[128,1,128]{2,0,1:T(8,128)}) %reduce-scatter.5.cloned.1.call-update) | async-done | bytes 65552 | tf_op jit(solution)/shard_map/reduce_scatter | solution.py:155
  358.2 119.1 %reduce-scatter.3.cloned.1.call-done = f32[128,1,128]{2,0,1:T(8,128)} async-done(((f32[4096,1,128]{2,0,1:T(8,128)}), f32[128,1,128]{2,0,1:T(8,128)}) %reduce-scatter.3.cloned.1.call-update) | async-done | bytes 65552 | tf_op jit(solution)/shard_map/reduce_scatter | solution.py:154
  478.8 4.0 all-to-all-start.5
  483.5 6.2 %all-to-all-done.5 = bf16[128,1,2,128]{3,2,1,0:T(2,128)(2,1)S(1)} async-done(((bf16[128,1,2,128]{3,2,1,0:T(2,128)(2,1)}), bf16[128,1,2,128]{3,2,1,0:T(2,128)(2,1)S(1)}, u32[]{:S(2)}, u32[]{:S(2)}) %all-to-all-start.5) | async-done | bytes 65568 | tf_op jit(solution)/shard_map/all_to_all | solution.py:160
  (160 shorter events, 63.2 us)
Async XLA Ops:
  7.2 46.8 %copy-start.4 = (s32[64]{0:T(128)S(1)}, s32[64]{0:T(128)}, u32[]{:S(2)}) copy-start(s32[64]{0:T(128)} %param.15) | copy-start | bytes 772
  8.5 16.0 %all-to-all-start = ((bf16[8,16,128]{2,0,1:T(8,128)(2,1)}), bf16[8,16,128]{2,0,1:T(8,128)(2,1)S(1)}, u32[]{:S(2)}, u32[]{:S(2)}) async-start(bf16[8,16,128]{2,0,1:T(8,128)(2,1)} %bitcast.43), calls=%async_computation | async-start | bytes 65536 | tf_op jit(solution)/shard_map/all_to_all | solution.py:35
  24.6 4.2 copy-start.3
  25.2 10.3 %all-to-all-start.2 = ((bf16[8,16,128]{2,0,1:T(8,128)(2,1)}), bf16[8,16,128]{2,0,1:T(8,128)(2,1)S(1)}, u32[]{:S(2)}, u32[]{:S(2)}) async-start(bf16[8,16,128]{2,0,1:T(8,128)(2,1)} %bitcast.54), calls=%async_computation.2 | async-start | bytes 65536 | tf_op jit(solution)/shard_map/all_to_all | solution.py:36
  28.7 79.9 %all-gather.3.cloned.1.call-start = ((), (), s32[]{:S(2)}) async-start(), calls=%async_computation.8 | async-start | bytes 1081344 | tf_op jit(solution)/shard_map/all_gather | solution.py:45
  35.5 18.6 %copy-start.2 = (bf16[8,16,128]{2,0,1:T(8,128)(2,1)}, bf16[8,16,128]{2,0,1:T(8,128)(2,1)S(1)}, u32[]{:S(2)}) copy-start(bf16[8,16,128]{2,0,1:T(8,128)(2,1)S(1)} %all-to-all-done.2) | copy-start | bytes 98308
  35.5 11.5 %all-to-all-start.1 = ((bf16[8,128,128]{2,0,1:T(8,128)(2,1)}), bf16[8,128,128]{2,0,1:T(8,128)(2,1)S(1)}, u32[]{:S(2)}, u32[]{:S(2)}) async-start(bf16[8,128,128]{2,0,1:T(8,128)(2,1)} %copy.64), calls=%async_computation.1 | async-start | bytes 524288 | tf_op jit(solution)/shard_map/all_to_all | solution.py:33
  47.0 11.5 %all-to-all-start.3 = ((bf16[8,128,128]{2,0,1:T(8,128)(2,1)}), bf16[8,128,128]{2,0,1:T(8,128)(2,1)S(1)}, u32[]{:S(2)}, u32[]{:S(2)}) async-start(bf16[8,128,128]{2,0,1:T(8,128)(2,1)} %copy.67), calls=%async_computation.3 | async-start | bytes 524288 | tf_op jit(solution)/shard_map/all_to_all | solution.py:34
  50.6 126.8 %all-gather.5.cloned.1.call-start = ((), (), s32[]{:S(2)}) async-start(), calls=%async_computation.9 | async-start | bytes 1081344 | tf_op jit(solution)/shard_map/all_gather | solution.py:46
  54.2 303.2 %reduce-scatter.5.cloned.1.call-start = ((), (), s32[]{:S(2)}) async-start(), calls=%async_computation.11 | async-start | bytes 2162688 | tf_op jit(solution)/shard_map/reduce_scatter | solution.py:155
  187.0 1.0 copy-start
  187.0 1.3 copy-start.1
  229.2 248.0 %reduce-scatter.3.cloned.1.call-start = ((), (), s32[]{:S(2)}) async-start(), calls=%async_computation.10 | async-start | bytes 2162688 | tf_op jit(solution)/shard_map/reduce_scatter | solution.py:154
  232.3 246.5 %all-to-all-start.4 = ((bf16[128,8,128]{2,1,0:T(8,128)(2,1)}), bf16[128,8,128]{2,1,0:T(8,128)(2,1)S(1)}, u32[]{:S(2)}, u32[]{:S(2)}) async-start(bf16[128,8,128]{2,1,0:T(8,128)(2,1)} %fusion.53), calls=%async_computation.4 | async-start | bytes 524288 | tf_op jit(solution)/shard_map/all_to_all | solution.py:159
  478.8 11.0 %all-to-all-start.5 = ((bf16[128,1,2,128]{3,2,1,0:T(2,128)(2,1)}), bf16[128,1,2,128]{3,2,1,0:T(2,128)(2,1)S(1)}, u32[]{:S(2)}, u32[]{:S(2)}) async-start(bf16[128,1,2,128]{3,2,1,0:T(2,128)(2,1)} %copy.71), calls=%async_computation.7 | async-start | bytes 131072 | tf_op jit(solution)/shard_map/all_to_all | solution.py:160
Sparse Core Ops, SparseCore 0:
  32.7 75.9 all-gather.2
  111.8 65.4 all-gather.4
  229.4 127.9 reduce-scatter.4
  361.6 115.5 reduce-scatter.2
where the time goes:
time: 501 us; the launch traced here: 498 us
  waiting for transfers between devices  376 us (75%)
  matrix products  42.7 us (9%)
  starting transfers between devices  28.4 us (6%)
  local copies, waits for them, and re-layouts  23.1 us (5%)
  between operations  16.7 us (3%)
  other arithmetic  9.68 us (2%)
    reduce_scatter x1, waiting for transfers between devices, on_device(): lax.psum_scatter(dv_term, 'blk', scatter_dimension=0, tiled=True)  121 us
    reduce_scatter x1, waiting for transfers between devices, on_device(): lax.psum_scatter(dk_term, 'blk', scatter_dimension=0, tiled=True)  119 us
    all_gather x1, waiting for transfers between devices, on_device(): lax.all_gather(v_local, 'blk', axis=0, tiled=True)  59.5 us
    all_gather x1, waiting for transfers between devices, on_device(): lax.all_gather(k_local, 'blk', axis=0, tiled=True)  50.1 us
    dot_general x12, matrix products, scored(): jnp.einsum('qkgd,tkd->kgqt', queries, key_blk, preferred_element_type=jnp...  11.5 us
  transfers between devices with their start and end apart: 10, of which 9 were waited for; matrix products, arithmetic and copies ran while one was open for 4% of the time, Pallas kernels for 0%

commit v1 on v0

v1 whole, which is shorter than its diff:
```python
import functools

import jax
import jax.numpy as jnp
from jax import lax
from jax.experimental import pallas as pl
from jax.experimental.pallas import tpu as pltpu
from jax.sharding import PartitionSpec as P

MESH = pl.DeviceIdType.MESH
F32 = jnp.float32
BF16 = jnp.bfloat16
NX, NY, NZ = 4, 4, 16
PLANE = NX * NY
RIGHT = NZ // 2
LEFT = NZ - 1 - RIGHT
TOK = 8
GROUP = 16
DH = 128
SEQ = 4096
BLOCKS = 64
ROWS = 1024
TILES = 4
TR = ROWS // TILES
KC = 512
SCALE = DH ** -0.5


def place():
    blk = lax.axis_index("blk")
    head = lax.axis_index("head")
    z = (blk // 8) * 4 + head % 4
    return (blk // 2) % 4, head // 4, z, blk % 2


def device(x, y, z, c):
    return (((z // 4) * 4 + x) * 2 + c, y * 4 + z % 4)


def kv_head(x, y):
    return (y // 2) * 4 + (x % 2) * 2 + y % 2


def group_peer(x, m):
    return (x // 2) * 2 + (m // 2) % 2, (m // 4) * 2 + m % 2


def meet(x, y, z, c):
    barrier = pltpu.get_barrier_semaphore()
    i = x * NY + y
    for d in range(1, PLANE):
        j = (i + d) % PLANE
        pl.semaphore_signal(barrier, inc=1, device_id=device(j // NY, j % NY, z, c), device_id_type=MESH)
    for to in (device(x, y, (z + 1) % NZ, c), device(x, y, (z + NZ - 1) % NZ, c), device(x, y, z, 1 - c)):
        pl.semaphore_signal(barrier, inc=1, device_id=to, device_id_type=MESH)
    pl.semaphore_wait(barrier, PLANE - 1 + 3)


def send(src, dst, send_sem, recv_sem, to):
    copy = pltpu.make_async_remote_copy(
        src_ref=src, dst_ref=dst, send_sem=send_sem, recv_sem=recv_sem, device_id=to, device_id_type=MESH
    )
    return copy


def gather_kernel(q_ref, g_ref, kv_ref, qg_ref, gg_ref, kvg_ref, q_s, q_r, g_s, g_r, p_s, p_r, r_s, r_r, l_s, l_r, c_s, c_r, own):
    x, y, z, c = place()
    i = x * NY + y
    m = kv_head(x, y)
    right = device(x, y, (z + 1) % NZ, c)
    left = device(x, y, (z + NZ - 1) % NZ, c)
    other = device(x, y, z, 1 - c)
    meet(x, y, z, c)
    sends = []

    def start(src, dst, ss, rs, to):
        copy = send(src, dst, ss, rs, to)
        copy.start()
        sends.append(copy)

    for d in range(1, PLANE):
        j = (i + d) % PLANE
        start(kv_ref.at[kv_head(j // NY, j % NY)], kvg_ref.at[z, c, i], p_s.at[d], p_r.at[d], device(j // NY, j % NY, z, c))
    kv_own = pltpu.make_async_copy(kv_ref.at[m], kvg_ref.at[z, c, i], own.at[0])
    kv_own.start()
    q_own = pltpu.make_async_copy(q_ref.at[:, pl.ds(m * GROUP, GROUP), :], qg_ref.at[m], own.at[1])
    g_own = pltpu.make_async_copy(g_ref.at[:, pl.ds(m * GROUP, GROUP), :], gg_ref.at[m], own.at[2])
    q_own.start()
    g_own.start()
    for d in range(1, 8):
        n = (m + d) % 8
        px, py = group_peer(x, n)
        to = device(px, py, z, c)
        start(q_ref.at[:, pl.ds(n * GROUP, GROUP), :], qg_ref.at[m], q_s.at[d], q_r.at[d], to)
        start(g_ref.at[:, pl.ds(n * GROUP, GROUP), :], gg_ref.at[m], g_s.at[d], g_r.at[d], to)

    kv_own.wait()
    for d in range(1, PLANE):
        j = (i + PLANE - d) % PLANE
        send(kv_ref.at[0], kvg_ref.at[z, c, j], p_s.at[d], p_r.at[d], other).wait_recv()

    for k in range(RIGHT + 1):
        zr = (z + NZ - k) % NZ
        if k:
            send(kvg_ref.at[zr, c], kvg_ref.at[zr, c], r_s.at[k - 1], r_r.at[k - 1], right).wait_recv()
        if k < RIGHT:
            start(kvg_ref.at[zr, c], kvg_ref.at[zr, c], r_s.at[k], r_r.at[k], right)
        start(kvg_ref.at[zr, c], kvg_ref.at[zr, c], c_s.at[k], c_r.at[k], other)
        if k <= LEFT:
            zl = (z + k) % NZ
            if k:
                send(kvg_ref.at[zl, c], kvg_ref.at[zl, c], l_s.at[k - 1], l_r.at[k - 1], left).wait_recv()
            if k < LEFT:
                start(kvg_ref.at[zl, c], kvg_ref.at[zl, c], l_s.at[k], l_r.at[k], left)
            if k:
                start(kvg_ref.at[zl, c], kvg_ref.at[zl, c], c_s.at[RIGHT + k], c_r.at[RIGHT + k], other)

    q_own.wait()
    g_own.wait()
    for d in range(1, 8):
        n = (m + 8 - d) % 8
        send(qg_ref.at[n], qg_ref.at[n], q_s.at[d], q_r.at[d], other).wait_recv()
        send(gg_ref.at[n], gg_ref.at[n], g_s.at[d], g_r.at[d], other).wait_recv()
    for k in range(NZ):
        zk = (z + NZ - k) % NZ if k <= RIGHT else (z + k - RIGHT) % NZ
        send(kvg_ref.at[zk, 1 - c], kvg_ref.at[zk, 1 - c], c_s.at[k], c_r.at[k], other).wait_recv()
    for copy in sends:
        copy.wait_send()


def gather(q, g, kv):
    sem = pltpu.SemaphoreType.DMA
    return pl.pallas_call(
        gather_kernel,
        out_shape=(
            jax.ShapeDtypeStruct((8, TOK, GROUP, DH), BF16),
            jax.ShapeDtypeStruct((8, TOK, GROUP, DH), BF16),
            jax.ShapeDtypeStruct((NZ, 2, PLANE, 16, DH), BF16),
        ),
        in_specs=[pl.BlockSpec(memory_space=pltpu.VMEM)] * 3,
        out_specs=[pl.BlockSpec(memory_space=pltpu.VMEM)] * 3,
        scratch_shapes=[
            sem((8,)), sem((8,)), sem((8,)), sem((8,)), sem((PLANE,)), sem((PLANE,)),
            sem((RIGHT,)), sem((RIGHT,)), sem((LEFT,)), sem((LEFT,)), sem((NZ,)), sem((NZ,)), sem((3,)),
        ],
        compiler_params=pltpu.CompilerParams(collective_id=0, has_side_effects=True, vmem_limit_bytes=32 << 20),
        name="gather_qkv",
    )(q, g, kv)


def dot(a, b, dims):
    return lax.dot_general(a, b, (dims, ((), ())), preferred_element_type=F32)


def attend_kernel(order_ref, inv_ref, q_ref, g_ref, kvg_ref, dq_ref, dkv_ref, ks, kt, vs, s_ref, dp_ref, dk, dv):
    x, y, z, c = place()

    def sort_block(p, carry):
        sb = inv_ref[p]
        b = sb // 2
        tiles = []
        for yy in range(2):
            for lo in range(4):
                tiles.append(kvg_ref[(b // 8) * 4 + lo, b % 2, ((b // 2) % 4) * NY + (sb % 2) * 2 + yy])
        both = jnp.stack(tiles).astype(F32).reshape(8, 2, 8, DH)
        rows = pl.ds(pl.multiple_of(p * 64, 64), 64)
        ks[rows, :] = both[:, 0].reshape(64, DH).astype(BF16)
        vs[rows, :] = both[:, 1].reshape(64, DH).astype(BF16)
        return carry

    lax.fori_loop(0, BLOCKS, sort_block, 0)
    for n in range(SEQ // KC):
        kt[:, n * KC:(n + 1) * KC] = ks[n * KC:(n + 1) * KC, :].T
    dk[...] = jnp.zeros_like(dk)
    dv[...] = jnp.zeros_like(dv)

    for t in range(TILES):
        sb = ((z // 4 * 4 + (x // 2) * 2 + t % 2) * 2 + c) * 2 + t // 2
        pos = order_ref[sb]
        count = pos // (KC // 64) + 1
        q = q_ref[t * TR:(t + 1) * TR, :]
        g = g_ref[t * TR:(t + 1) * TR, :]
        qt = q.T
        gt = g.T
        lane = lax.broadcasted_iota(jnp.int32, (1, TR), 1)
        limit = pos * 64 + (lane // 128) * 32 + (z % 4) * 8 + (lane // 16) % 8

        def scores(n, top):
            rows = pl.ds(pl.multiple_of(n * KC, KC), KC)
            s = dot(ks[rows, :], qt, ((1,), (0,)))
            key_pos = n * KC + lax.broadcasted_iota(jnp.int32, (KC, TR), 0)
            s = jnp.where(key_pos <= limit, s, -1e30)
            s_ref[rows, :] = s
            dp_ref[rows, :] = dot(vs[rows, :], gt, ((1,), (0,)))
            return jnp.maximum(top, jnp.max(s.reshape(KC // 8, 8, TR), axis=0))

        top = lax.fori_loop(0, count, scores, jnp.full((8, TR), -1e30, F32))
        top = jnp.max(top, axis=0, keepdims=True)

        def weigh(n, carry):
            total, mixed = carry
            rows = pl.ds(pl.multiple_of(n * KC, KC), KC)
            e = jnp.exp((s_ref[rows, :] - top) * SCALE)
            s_ref[rows, :] = e
            total = total + jnp.sum(e.reshape(KC // 8, 8, TR), axis=0)
            mixed = mixed + jnp.sum((e * dp_ref[rows, :]).reshape(KC // 8, 8, TR), axis=0)
            return total, mixed

        zero = jnp.zeros((8, TR), F32)
        total, mixed = lax.fori_loop(0, count, weigh, (zero, zero))
        inverse = 1.0 / jnp.sum(total, axis=0, keepdims=True)
        delta = jnp.sum(mixed, axis=0, keepdims=True) * inverse

        def grads(n, dqt):
            rows = pl.ds(pl.multiple_of(n * KC, KC), KC)
            p = s_ref[rows, :] * inverse
            ds = (p * (dp_ref[rows, :] - delta)).astype(BF16)
            dv[rows, :] += dot(p.astype(BF16), g, ((1,), (0,)))
            dk[rows, :] += dot(ds, q, ((1,), (0,)))
            return dqt + dot(kt[:, rows], ds, ((1,), (0,)))

        dqt = lax.fori_loop(0, count, grads, jnp.zeros((DH, TR), F32))
        dq_ref[t * TR:(t + 1) * TR, :] = (dqt * SCALE).T.astype(BF16)

    def spread_block(sb, carry):
        p = order_ref[sb]
        b = sb // 2
        rows = pl.ds(pl.multiple_of(p * 64, 64), 64)
        both = jnp.stack([(dk[rows, :] * SCALE).reshape(8, 8, DH), dv[rows, :].reshape(8, 8, DH)], axis=1)
        tiles = both.reshape(8, 16, DH).astype(BF16)
        for yy in range(2):
            for lo in range(4):
                dkv_ref[(b // 8) * 4 + lo, b % 2, ((b // 2) % 4) * NY + (sb % 2) * 2 + yy] = tiles[yy * 4 + lo]
        return carry

    lax.fori_loop(0, BLOCKS, spread_block, 0)


def attend(order, inverse, q, g, kvg):
    vmem = pl.BlockSpec(memory_space=pltpu.VMEM)
    smem = pl.BlockSpec(memory_space=pltpu.SMEM)
    return pl.pallas_call(
        attend_kernel,
        out_shape=(
            jax.ShapeDtypeStruct((ROWS, DH), BF16),
            jax.ShapeDtypeStruct((NZ, 2, PLANE, 16, DH), BF16),
        ),
        in_specs=[smem, smem, vmem, vmem, vmem],
        out_specs=[vmem, vmem],
        scratch_shapes=[
            pltpu.VMEM((SEQ, DH), BF16),
            pltpu.VMEM((DH, SEQ), BF16),
            pltpu.VMEM((SEQ, DH), BF16),
            pltpu.VMEM((SEQ, TR), F32),
            pltpu.VMEM((SEQ, TR), F32),
            pltpu.VMEM((SEQ, DH), F32),
            pltpu.VMEM((SEQ, DH), F32),
        ],
        compiler_params=pltpu.CompilerParams(vmem_limit_bytes=48 << 20),
        name="attend",
    )(order, inverse, q, g, kvg)


def reduce_kernel(dq_ref, dkv_ref, dqh_ref, dkvh_ref, cx, rr, rst, lr, lst, fin, fst, q_s, q_r, p_s, p_r, r_s, r_r, l_s, l_r, c_s, c_r, own):
    x, y, z, c = place()
    i = x * NY + y
    m = kv_head(x, y)
    right = device(x, y, (z + 1) % NZ, c)
    left = device(x, y, (z + NZ - 1) % NZ, c)
    other = device(x, y, z, 1 - c)
    meet(x, y, z, c)
    sends = []

    def start(src, dst, ss, rs, to):
        copy = send(src, dst, ss, rs, to)
        copy.start()
        sends.append(copy)

    order = []
    for k in range(RIGHT):
        order.append((z + RIGHT - k) % NZ)
        if k < LEFT:
            order.append((z + NZ - LEFT + k) % NZ)
    order.append(z)
    for n, dest in enumerate(order):
        start(dkv_ref.at[dest, 1 - c], cx.at[dest], c_s.at[n], c_r.at[n], other)
    q_own = pltpu.make_async_copy(dq_ref.at[m], dqh_ref.at[:, pl.ds(m * GROUP, GROUP), :], own.at[0])
    q_own.start()
    for d in range(1, 8):
        n = (m + d) % 8
        px, py = group_peer(x, n)
        start(dq_ref.at[n], dqh_ref.at[:, pl.ds(m * GROUP, GROUP), :], q_s.at[d], q_r.at[d], device(px, py, z, c))

    def mine(n):
        dest = order[n]
        send(cx.at[dest], cx.at[dest], c_s.at[n], c_r.at[n], other).wait_recv()
        return dkv_ref[dest, c].astype(F32) + cx[dest].astype(F32)

    n = 0
    for k in range(RIGHT):
        total = mine(n)
        n += 1
        if k:
            send(rr.at[k - 1], rr.at[k - 1], r_s.at[k - 1], r_r.at[k - 1], right).wait_recv()
            total = total + rr[k - 1].astype(F32)
        rst[k] = total.astype(BF16)
        start(rst.at[k], rr.at[k], r_s.at[k], r_r.at[k], right)
        if k < LEFT:
            total = mine(n)
            n += 1
            if k:
                send(lr.at[k - 1], lr.at[k - 1], l_s.at[k - 1], l_r.at[k - 1], left).wait_recv()
                total = total + lr[k - 1].astype(F32)
            lst[k] = total.astype(BF16)
            start(lst.at[k], lr.at[k], l_s.at[k], l_r.at[k], left)
    total = mine(n)
    send(lr.at[LEFT - 1], lr.at[LEFT - 1], l_s.at[LEFT - 1], l_r.at[LEFT - 1], left).wait_recv()
    total = total + lr[LEFT - 1].astype(F32)
    send(rr.at[RIGHT - 1], rr.at[RIGHT - 1], r_s.at[RIGHT - 1], r_r.at[RIGHT - 1], right).wait_recv()
    total = total + rr[RIGHT - 1].astype(F32)
    fst[...] = total.astype(BF16)
    for d in range(1, PLANE):
        j = (i + d) % PLANE
        start(fst.at[j], fin.at[i], p_s.at[d], p_r.at[d], device(j // NY, j % NY, z, c))
    p_own = pltpu.make_async_copy(fst.at[i], fin.at[i], own.at[1])
    p_own.start()
    p_own.wait()
    for d in range(1, PLANE):
        j = (i + PLANE - d) % PLANE
        send(fin.at[j], fin.at[j], p_s.at[d], p_r.at[d], other).wait_recv()
    for n in range(8):
        px, py = (n // 2) % 2, (n // 4) * 2 + n % 2
        total = fin[px * NY + py].astype(F32) + fin[(px + 2) * NY + py].astype(F32)
        dkvh_ref[n] = total.astype(BF16)
    q_own.wait()
    for d in range(1, 8):
        n = (m + 8 - d) % 8
        send(dq_ref.at[n], dqh_ref.at[:, pl.ds(n * GROUP, GROUP), :], q_s.at[d], q_r.at[d], other).wait_recv()
    for copy in sends:
        copy.wait_send()


def reduce(dq, dkv):
    sem = pltpu.SemaphoreType.DMA
    block = (PLANE, 16, DH)
    return pl.pallas_call(
        reduce_kernel,
        out_shape=(
            jax.ShapeDtypeStruct((TOK, 8 * GROUP, DH), BF16),
            jax.ShapeDtypeStruct((8, 16, DH), BF16),
        ),
        in_specs=[pl.BlockSpec(memory_space=pltpu.VMEM)] * 2,
        out_specs=[pl.BlockSpec(memory_space=pltpu.VMEM)] * 2,
        scratch_shapes=[
            pltpu.VMEM((NZ,) + block, BF16),
            pltpu.VMEM((RIGHT,) + block, BF16),
            pltpu.VMEM((RIGHT,) + block, BF16),
            pltpu.VMEM((LEFT,) + block, BF16),
            pltpu.VMEM((LEFT,) + block, BF16),
            pltpu.VMEM(block, BF16),
            pltpu.VMEM(block, BF16),
            sem((8,)), sem((8,)), sem((PLANE,)), sem((PLANE,)),
            sem((RIGHT,)), sem((RIGHT,)), sem((LEFT,)), sem((LEFT,)), sem((NZ,)), sem((NZ,)), sem((2,)),
        ],
        compiler_params=pltpu.CompilerParams(collective_id=1, has_side_effects=True, vmem_limit_bytes=32 << 20),
        name="reduce_grads",
    )(dq, dkv)


def on_device(query, key, value, out_grad, block_order):
    kv = jnp.concatenate((jnp.transpose(key, (1, 0, 2)), jnp.transpose(value, (1, 0, 2))), axis=1)
    q, g, kvg = gather(query, out_grad, kv)
    slots = jnp.arange(BLOCKS, dtype=jnp.int32)
    inverse = jnp.sum(jnp.where(block_order[None, :] == slots[:, None], slots[None, :], 0), axis=1)
    dq, dkv = attend(block_order, inverse, q.reshape(ROWS, DH), g.reshape(ROWS, DH), kvg)
    dq_home, dkv_home = reduce(dq.reshape(8, TOK, GROUP, DH), dkv)
    grads = jnp.transpose(dkv_home, (1, 0, 2))
    return dq_home, grads[:TOK], grads[TOK:]


def solution(mesh):
    rows = P(("blk", "head"), None, None)
    return jax.shard_map(
        on_device, mesh=mesh, in_specs=(rows,) * 4 + (P(),), out_specs=(rows,) * 3, check_vma=False
    )
```

time: 501 us -> 121 us (0.24)
  the two profiles are of different devices: /device:TPU:1 before, /device:TPU:24 now
where the time goes in v1:
time: 121 us
  Pallas kernels  114 us (94%)
  local copies, waits for them, and re-layouts  5.22 us (4%)
    pallas_call x1, Pallas kernels, gather(): pl.pallas_call(gather_kernel, out_shape=(jax.ShapeDtypeStruct((8, TOK, GR...  50.6 us
    pallas_call x1, Pallas kernels, reduce(): pl.pallas_call(reduce_kernel, out_shape=(jax.ShapeDtypeStruct((TOK, 8 * G...  49 us
    pallas_call x1, Pallas kernels, attend(): pl.pallas_call(attend_kernel, out_shape=(jax.ShapeDtypeStruct((ROWS, DH),...  14.4 us
    unnamed x9, local copies, waits for them, and re-layouts  4.47 us

profile of v1, /device:TPU:24, one launch (start us, length us, event | category | flops | bytes accessed | tf_op | source)
XLA Modules:
  0.0 120.7 jit_solution(6290428770960040725)
XLA Ops:
  0.6 0.8 select_reduce_fusion.inv_ref
  1.4 0.8 copy_bitcast_fusion
  2.2 0.0 copy-start
  2.2 0.9 copy-done
  3.1 0.0 copy-start.1
  3.1 0.9 copy-done.1
  4.1 50.6 %gather_qkv.1 = (bf16[8,8,16,128]{3,2,1,0:T(8,128)(2,1)S(1)}, bf16[8,8,16,128]{3,2,1,0:T(8,128)(2,1)S(1)}, bf16[16,2,16,16,128]{4,3,2,1,0:T(8,128)(2,1)S(1)}) custom-call(bf16[8,128,128]{2,1,0:T(8,128)(2,1)S(1)} %copy-done, bf16[8,128,128]{2,1,0:T(8,128)(2,1)S(1)} %copy-done.1, bf16[8,16,128]{2,1,0:T(8,128)(2,1)S(1)} %pad_maximum_fusion.kv_ref), custom_call_target="tpu_custom_call" | custom-call | tf_op jit(solution)/shard_map/gather_qkv/pallas_call | solution.py:133
  54.7 0.0 copy-start.2
  54.7 0.6 copy-done.2
  55.3 14.4 %attend.1 = (bf16[1024,128]{1,0:T(8,128)(2,1)S(1)}, bf16[16,2,16,16,128]{4,3,2,1,0:T(8,128)(2,1)S(1)}) custom-call(s32[64]{0:T(128)S(1)} %copy-done.2, s32[64]{0:T(128)S(1)} %select_reduce_fusion.inv_ref, bf16[1024,128]{1,0:T(8,128)(2,1)S(1)} %bitcast.9, bf16[1024,128]{1,0:T(8,128)(2,1)S(1)} %bitcast.10, ...), custom_call_target="tpu_custom_call" | custom-call | tf_op jit(solution)/shard_map/attend/pallas_call | solution.py:242
  69.8 49.0 %reduce_grads.1 = (bf16[8,128,128]{2,1,0:T(8,128)(2,1)S(1)}, bf16[8,16,128]{2,1,0:T(8,128)(2,1)S(1)}) custom-call(bf16[8,8,16,128]{3,2,1,0:T(8,128)(2,1)S(1)} %bitcast.8, bf16[16,2,16,16,128]{4,3,2,1,0:T(8,128)(2,1)S(1)} %get-tuple-element.14.dkv_ref), custom_call_target="tpu_custom_call" | custom-call | tf_op jit(solution)/shard_map/reduce_grads/pallas_call | solution.py:346
  118.7 0.6 copy.15
  119.4 0.6 copy.14
  120.0 0.7 copy.19
  (2 shorter events, 0.0 us)
Async XLA Ops:
  2.2 1.0 copy-start
  3.1 0.9 copy-start.1
  54.7 0.7 copy-start.2

commit v2 on v1

v2 whole, which is shorter than its diff:
```python
import jax
import jax.numpy as jnp
from jax import lax
from jax.experimental import pallas as pl
from jax.experimental.pallas import tpu as pltpu
from jax.sharding import PartitionSpec as P

MESH = pl.DeviceIdType.MESH
F32 = jnp.float32
BF16 = jnp.bfloat16
NX, NY, NZ = 4, 4, 16
NQ = NZ // 2
PEERS = 8
TOK = 8
GROUP = 16
DH = 128
SEQ = 4096
BLOCKS = 64
ROWS = 1024
TILES = 4
TR = ROWS // TILES
KC = 512
SCALE = DH ** -0.5


def place():
    blk = lax.axis_index("blk")
    head = lax.axis_index("head")
    z = (blk // 8) * 4 + head % 4
    return (blk // 2) % 4, head // 4, z, blk % 2


def device(x, y, z, c):
    return (((z // 4) * 4 + x) * 2 + c, y * 4 + z % 4)


def peer(x, z, c, n):
    return device(x, n // 2, (z // 2) * 2 + n % 2, c)


def meet(x, y, z, c):
    barrier = pltpu.get_barrier_semaphore()
    m = y * 2 + z % 2
    to = [peer(x, z, c, (m + d) % PEERS) for d in range(1, PEERS)]
    to += [device(x, y, (z + 2 * d) % NZ, c) for d in range(1, NQ)]
    to += [device((x + d) % NX, y, z, c) for d in range(1, NX)]
    to += [device(x, y, z, 1 - c)]
    for one in to:
        pl.semaphore_signal(barrier, inc=1, device_id=one, device_id_type=MESH)
    pl.semaphore_wait(barrier, len(to))


def send(src, dst, send_sem, recv_sem, to):
    copy = pltpu.make_async_remote_copy(
        src_ref=src, dst_ref=dst, send_sem=send_sem, recv_sem=recv_sem, device_id=to, device_id_type=MESH
    )
    return copy


Z_ORDER = (1, 7, 2, 6, 3, 5, 4)
X_ORDER = (1, 3, 2)


def gather_kernel(q_ref, g_ref, kv_ref, qg_ref, gg_ref, kvg_ref, q_s, q_r, g_s, g_r, p_s, p_r, z_s, z_r, x_s, x_r, c_s, c_r, own):
    x, y, z, c = place()
    m = y * 2 + z % 2
    zq = z // 2
    other = device(x, y, z, 1 - c)
    meet(x, y, z, c)
    sends = []

    def start(src, dst, ss, rs, to):
        copy = send(src, dst, ss, rs, to)
        copy.start()
        sends.append(copy)

    def arrived(dst, ss, rs):
        send(dst, dst, ss, rs, other).wait_recv()

    for d in range(1, PEERS):
        n = (m + d) % PEERS
        start(kv_ref.at[n], kvg_ref.at[zq, x, c, m], p_s.at[d], p_r.at[d], peer(x, z, c, n))
    kv_own = pltpu.make_async_copy(kv_ref.at[m], kvg_ref.at[zq, x, c, m], own.at[0])
    kv_own.start()
    q_own = pltpu.make_async_copy(q_ref.at[:, pl.ds(m * GROUP, GROUP), :], qg_ref.at[m], own.at[1])
    g_own = pltpu.make_async_copy(g_ref.at[:, pl.ds(m * GROUP, GROUP), :], gg_ref.at[m], own.at[2])
    q_own.start()
    g_own.start()
    kv_own.wait()
    for d in range(1, PEERS):
        n = (m + PEERS - d) % PEERS
        arrived(kvg_ref.at[zq, x, c, n], p_s.at[d], p_r.at[d])
    block = kvg_ref.at[zq, x, c]
    for d in Z_ORDER:
        start(block, block, z_s.at[d], z_r.at[d], device(x, y, (z + 2 * d) % NZ, c))

    def share(d):
        block = kvg_ref.at[(zq + NQ - d) % NQ, x, c]
        for e in X_ORDER:
            start(block, block, x_s.at[d, e], x_r.at[d, e], device((x + e) % NX, y, z, c))

    def swap(d):
        zk = (zq + NQ - d) % NQ
        for e in X_ORDER:
            arrived(kvg_ref.at[zk, (x + NX - e) % NX, c], x_s.at[d, e], x_r.at[d, e])
        start(kvg_ref.at[zk, :, c], kvg_ref.at[zk, :, c], c_s.at[d], c_r.at[d], other)

    share(0)
    for d in range(1, PEERS):
        n = (m + d) % PEERS
        to = peer(x, z, c, n)
        start(q_ref.at[:, pl.ds(n * GROUP, GROUP), :], qg_ref.at[m], q_s.at[d], q_r.at[d], to)
        start(g_ref.at[:, pl.ds(n * GROUP, GROUP), :], gg_ref.at[m], g_s.at[d], g_r.at[d], to)
    for d in Z_ORDER:
        arrived(kvg_ref.at[(zq + NQ - d) % NQ, x, c], z_s.at[d], z_r.at[d])
        share(d)
    for d in (0,) + Z_ORDER:
        swap(d)
    q_own.wait()
    g_own.wait()
    for d in range(1, PEERS):
        n = (m + PEERS - d) % PEERS
        arrived(qg_ref.at[n], q_s.at[d], q_r.at[d])
        arrived(gg_ref.at[n], g_s.at[d], g_r.at[d])
    for d in range(NQ):
        arrived(kvg_ref.at[(zq + NQ - d) % NQ, :, 1 - c], c_s.at[d], c_r.at[d])
    for copy in sends:
        copy.wait_send()


def gather(q, g, kv):
    sem = pltpu.SemaphoreType.DMA
    return pl.pallas_call(
        gather_kernel,
        out_shape=(
            jax.ShapeDtypeStruct((PEERS, TOK, GROUP, DH), BF16),
            jax.ShapeDtypeStruct((PEERS, TOK, GROUP, DH), BF16),
            jax.ShapeDtypeStruct((NQ, NX, 2, PEERS, 16, DH), BF16),
        ),
        in_specs=[pl.BlockSpec(memory_space=pltpu.VMEM)] * 3,
        out_specs=[pl.BlockSpec(memory_space=pltpu.VMEM)] * 3,
        scratch_shapes=[sem((8,))] * 8 + [sem((NQ, NX))] * 2 + [sem((NQ,))] * 2 + [sem((3,))],
        compiler_params=pltpu.CompilerParams(collective_id=0, has_side_effects=True, vmem_limit_bytes=32 << 20),
        name="gather_qkv",
    )(q, g, kv)


def dot(a, b, dims):
    return lax.dot_general(a, b, (dims, ((), ())), preferred_element_type=F32)


def attend_kernel(order_ref, inv_ref, q_ref, g_ref, kvg_ref, dq_ref, dkv_ref, ks, kt, vs, s_ref, dp_ref, dk, dv):
    x, y, z, c = place()

    def sort_block(p, carry):
        sb = inv_ref[p]
        b = sb // 2
        tiles = []
        for yy in range(2):
            for lo in range(4):
                tiles.append(kvg_ref[(b // 8) * 2 + lo // 2, (b // 2) % 4, b % 2, ((sb % 2) * 2 + yy) * 2 + lo % 2])
        both = jnp.stack(tiles).astype(F32).reshape(8, 2, 8, DH)
        rows = pl.ds(pl.multiple_of(p * 64, 64), 64)
        ks[rows, :] = both[:, 0].reshape(64, DH).astype(BF16)
        vs[rows, :] = both[:, 1].reshape(64, DH).astype(BF16)
        return carry

    lax.fori_loop(0, BLOCKS, sort_block, 0)
    for n in range(SEQ // KC):
        kt[:, n * KC:(n + 1) * KC] = ks[n * KC:(n + 1) * KC, :].T
    dk[...] = jnp.zeros_like(dk)
    dv[...] = jnp.zeros_like(dv)

    for t in range(TILES):
        sb = ((z // 4 * 4 + x) * 2 + c) * 2 + t // 2
        pos = order_ref[sb]
        count = pos // (KC // 64) + 1
        q = q_ref[t * TR:(t + 1) * TR, :]
        g = g_ref[t * TR:(t + 1) * TR, :]
        qt = q.T
        gt = g.T
        lane = lax.broadcasted_iota(jnp.int32, (1, TR), 1)
        limit = pos * 64 + (t % 2) * 32 + (z % 4 // 2) * 16 + (lane // 128) * 8 + (lane // 16) % 8

        def scores(n, top):
            rows = pl.ds(pl.multiple_of(n * KC, KC), KC)
            s = dot(ks[rows, :], qt, ((1,), (0,)))
            key_pos = n * KC + lax.broadcasted_iota(jnp.int32, (KC, TR), 0)
            s = jnp.where(key_pos <= limit, s, -1e30)
            s_ref[rows, :] = s
            dp_ref[rows, :] = dot(vs[rows, :], gt, ((1,), (0,)))
            return jnp.maximum(top, jnp.max(s.reshape(KC // 8, 8, TR), axis=0))

        top = lax.fori_loop(0, count, scores, jnp.full((8, TR), -1e30, F32))
        top = jnp.max(top, axis=0, keepdims=True)

        def weigh(n, carry):
            total, mixed = carry
            rows = pl.ds(pl.multiple_of(n * KC, KC), KC)
            e = jnp.exp((s_ref[rows, :] - top) * SCALE)
            s_ref[rows, :] = e
            total = total + jnp.sum(e.reshape(KC // 8, 8, TR), axis=0)
            mixed = mixed + jnp.sum((e * dp_ref[rows, :]).reshape(KC // 8, 8, TR), axis=0)
            return total, mixed

        zero = jnp.zeros((8, TR), F32)
        total, mixed = lax.fori_loop(0, count, weigh, (zero, zero))
        inverse = 1.0 / jnp.sum(total, axis=0, keepdims=True)
        delta = jnp.sum(mixed, axis=0, keepdims=True) * inverse

        def grads(n, dqt):
            rows = pl.ds(pl.multiple_of(n * KC, KC), KC)
            p = s_ref[rows, :] * inverse
            ds = (p * (dp_ref[rows, :] - delta)).astype(BF16)
            dv[rows, :] += dot(p.astype(BF16), g, ((1,), (0,)))
            dk[rows, :] += dot(ds, q, ((1,), (0,)))
            return dqt + dot(kt[:, rows], ds, ((1,), (0,)))

        dqt = lax.fori_loop(0, count, grads, jnp.zeros((DH, TR), F32))
        dq_ref[t * TR:(t + 1) * TR, :] = (dqt * SCALE).T.astype(BF16)

    def spread_block(sb, carry):
        p = order_ref[sb]
        b = sb // 2
        rows = pl.ds(pl.multiple_of(p * 64, 64), 64)
        both = jnp.stack([(dk[rows, :] * SCALE).reshape(8, 8, DH), dv[rows, :].reshape(8, 8, DH)], axis=1)
        tiles = both.reshape(8, 16, DH).astype(BF16)
        for yy in range(2):
            for lo in range(4):
                dkv_ref[(b // 8) * 2 + lo // 2, (b // 2) % 4, b % 2, ((sb % 2) * 2 + yy) * 2 + lo % 2] = tiles[yy * 4 + lo]
        return carry

    lax.fori_loop(0, BLOCKS, spread_block, 0)


def attend(order, inverse, q, g, kvg):
    vmem = pl.BlockSpec(memory_space=pltpu.VMEM)
    smem = pl.BlockSpec(memory_space=pltpu.SMEM)
    return pl.pallas_call(
        attend_kernel,
        out_shape=(
            jax.ShapeDtypeStruct((ROWS, DH), BF16),
            jax.ShapeDtypeStruct((NQ, NX, 2, PEERS, 16, DH), BF16),
        ),
        in_specs=[smem, smem, vmem, vmem, vmem],
        out_specs=[vmem, vmem],
        scratch_shapes=[
            pltpu.VMEM((SEQ, DH), BF16),
            pltpu.VMEM((DH, SEQ), BF16),
            pltpu.VMEM((SEQ, DH), BF16),
            pltpu.VMEM((SEQ, TR), F32),
            pltpu.VMEM((SEQ, TR), F32),
            pltpu.VMEM((SEQ, DH), F32),
            pltpu.VMEM((SEQ, DH), F32),
        ],
        compiler_params=pltpu.CompilerParams(vmem_limit_bytes=48 << 20),
        name="attend",
    )(order, inverse, q, g, kvg)


def reduce_kernel(dq_ref, dkv_ref, dqh_ref, dkvh_ref, cx, xst, xr, zst, zr, fst, q_s, q_r, p_s, p_r, z_s, z_r, x_s, x_r, c_s, c_r, own):
    x, y, z, c = place()
    m = y * 2 + z % 2
    zq = z // 2
    other = device(x, y, z, 1 - c)
    meet(x, y, z, c)
    sends = []

    def start(src, dst, ss, rs, to):
        copy = send(src, dst, ss, rs, to)
        copy.start()
        sends.append(copy)

    def arrived(dst, ss, rs):
        send(dst, dst, ss, rs, other).wait_recv()

    order = Z_ORDER[::-1] + (0,)
    for d in order:
        zk = (zq + d) % NQ
        start(dkv_ref.at[zk, :, 1 - c], cx.at[d], c_s.at[d], c_r.at[d], other)
    q_own = pltpu.make_async_copy(dq_ref.at[m], dqh_ref.at[:, pl.ds(m * GROUP, GROUP), :], own.at[0])
    q_own.start()
    for d in order:
        zk = (zq + d) % NQ
        arrived(cx.at[d], c_s.at[d], c_r.at[d])
        for e in X_ORDER:
            xd = (x + e) % NX
            xst[d, e] = (dkv_ref[zk, xd, c].astype(F32) + cx[d, xd].astype(F32)).astype(BF16)
            start(xst.at[d, e], xr.at[d, e], x_s.at[d, e], x_r.at[d, e], device(xd, y, z, c))
    for d in range(1, PEERS):
        n = (m + d) % PEERS
        start(dq_ref.at[n], dqh_ref.at[:, pl.ds(m * GROUP, GROUP), :], q_s.at[d], q_r.at[d], peer(x, z, c, n))
    for d in order:
        zk = (zq + d) % NQ
        total = dkv_ref[zk, x, c].astype(F32) + cx[d, x].astype(F32)
        for e in X_ORDER:
            arrived(xr.at[d, e], x_s.at[d, e], x_r.at[d, e])
            total = total + xr[d, e].astype(F32)
        if d:
            zst[d] = total.astype(BF16)
            start(zst.at[d], zr.at[d], z_s.at[d], z_r.at[d], device(x, y, (z + 2 * d) % NZ, c))
    for d in Z_ORDER:
        arrived(zr.at[d], z_s.at[d], z_r.at[d])
        total = total + zr[d].astype(F32)
    fst[...] = total.astype(BF16)
    for d in range(1, PEERS):
        n = (m + d) % PEERS
        start(fst.at[n], dkvh_ref.at[m], p_s.at[d], p_r.at[d], peer(x, z, c, n))
    p_own = pltpu.make_async_copy(fst.at[m], dkvh_ref.at[m], own.at[1])
    p_own.start()
    q_own.wait()
    p_own.wait()
    for d in range(1, PEERS):
        n = (m + PEERS - d) % PEERS
        arrived(dqh_ref.at[:, pl.ds(n * GROUP, GROUP), :], q_s.at[d], q_r.at[d])
        arrived(dkvh_ref.at[n], p_s.at[d], p_r.at[d])
    for copy in sends:
        copy.wait_send()


def reduce(dq, dkv):
    sem = pltpu.SemaphoreType.DMA
    block = (PEERS, 16, DH)
    return pl.pallas_call(
        reduce_kernel,
        out_shape=(
            jax.ShapeDtypeStruct((TOK, 8 * GROUP, DH), BF16),
            jax.ShapeDtypeStruct((8, 16, DH), BF16),
        ),
        in_specs=[pl.BlockSpec(memory_space=pltpu.VMEM)] * 2,
        out_specs=[pl.BlockSpec(memory_space=pltpu.VMEM)] * 2,
        scratch_shapes=[
            pltpu.VMEM((NQ, NX) + block, BF16),
            pltpu.VMEM((NQ, NX) + block, BF16),
            pltpu.VMEM((NQ, NX) + block, BF16),
            pltpu.VMEM((NQ,) + block, BF16),
            pltpu.VMEM((NQ,) + block, BF16),
            pltpu.VMEM(block, BF16),
        ] + [sem((8,))] * 6 + [sem((NQ, NX))] * 2 + [sem((NQ,))] * 2 + [sem((2,))],
        compiler_params=pltpu.CompilerParams(collective_id=1, has_side_effects=True, vmem_limit_bytes=32 << 20),
        name="reduce_grads",
    )(dq, dkv)


def on_device(query, key, value, out_grad, block_order):
    kv = jnp.concatenate((jnp.transpose(key, (1, 0, 2)), jnp.transpose(value, (1, 0, 2))), axis=1)
    q, g, kvg = gather(query, out_grad, kv)
    slots = jnp.arange(BLOCKS, dtype=jnp.int32)
    inverse = jnp.sum(jnp.where(block_order[None, :] == slots[:, None], slots[None, :], 0), axis=1)
    dq, dkv = attend(block_order, inverse, q.reshape(ROWS, DH), g.reshape(ROWS, DH), kvg)
    dq_home, dkv_home = reduce(dq.reshape(8, TOK, GROUP, DH), dkv)
    grads = jnp.transpose(dkv_home, (1, 0, 2))
    return dq_home, grads[:TOK], grads[TOK:]


def solution(mesh):
    rows = P(("blk", "head"), None, None)
    return jax.shard_map(
        on_device, mesh=mesh, in_specs=(rows,) * 4 + (P(),), out_specs=(rows,) * 3, check_vma=False
    )
```

time: 121 us -> 108 us (0.89)
  the two profiles are of different devices: /device:TPU:24 before, /device:TPU:1 now
where the time goes in v2:
time: 108 us
  Pallas kernels  101 us (94%)
  local copies, waits for them, and re-layouts  5.22 us (5%)
    pallas_call x1, Pallas kernels, gather(): pl.pallas_call(gather_kernel, out_shape=(jax.ShapeDtypeStruct((PEERS, TOK...  43.4 us
    pallas_call x1, Pallas kernels, reduce(): pl.pallas_call(reduce_kernel, out_shape=(jax.ShapeDtypeStruct((TOK, 8 * G...  37.1 us
    pallas_call x1, Pallas kernels, attend(): pl.pallas_call(attend_kernel, out_shape=(jax.ShapeDtypeStruct((ROWS, DH),...  20.7 us
    unnamed x9, local copies, waits for them, and re-layouts  4.47 us

profile of v2, /device:TPU:1, one launch (start us, length us, event | category | flops | bytes accessed | tf_op | source)
XLA Modules:
  0.0 107.8 jit_solution(778783922082418671)
XLA Ops:
  0.6 0.8 select_reduce_fusion.inv_ref
  1.4 0.8 copy_bitcast_fusion
  2.2 0.0 copy-start
  2.2 0.9 copy-done
  3.1 0.0 copy-start.1
  3.1 0.9 copy-done.1
  4.1 43.4 %gather_qkv.1 = (bf16[8,8,16,128]{3,2,1,0:T(8,128)(2,1)S(1)}, bf16[8,8,16,128]{3,2,1,0:T(8,128)(2,1)S(1)}, bf16[8,4,2,8,16,128]{5,4,3,2,1,0:T(8,128)(2,1)S(1)}) custom-call(bf16[8,128,128]{2,1,0:T(8,128)(2,1)S(1)} %copy-done, bf16[8,128,128]{2,1,0:T(8,128)(2,1)S(1)} %copy-done.1, bf16[8,16,128]{2,1,0:T(8,128)(2,1)S(1)} %pad_maximum_fusion.kv_ref), custom_call_target="tpu_custom_call" | custom-call | tf_op jit(solution)/shard_map/gather_qkv/pallas_call | solution.py:133
  47.5 0.0 copy-start.2
  47.5 0.6 copy-done.2
  48.1 20.7 %attend.1 = (bf16[1024,128]{1,0:T(8,128)(2,1)S(1)}, bf16[8,4,2,8,16,128]{5,4,3,2,1,0:T(8,128)(2,1)S(1)}) custom-call(s32[64]{0:T(128)S(1)} %copy-done.2, s32[64]{0:T(128)S(1)} %select_reduce_fusion.inv_ref, bf16[1024,128]{1,0:T(8,128)(2,1)S(1)} %bitcast.9, bf16[1024,128]{1,0:T(8,128)(2,1)S(1)} %bitcast.10, ...), custom_call_target="tpu_custom_call" | custom-call | tf_op jit(solution)/shard_map/attend/pallas_call | solution.py:239
  68.8 37.1 %reduce_grads.1 = (bf16[8,128,128]{2,1,0:T(8,128)(2,1)S(1)}, bf16[8,16,128]{2,1,0:T(8,128)(2,1)S(1)}) custom-call(bf16[8,8,16,128]{3,2,1,0:T(8,128)(2,1)S(1)} %bitcast.8, bf16[8,4,2,8,16,128]{5,4,3,2,1,0:T(8,128)(2,1)S(1)} %get-tuple-element.14.dkv_ref), custom_call_target="tpu_custom_call" | custom-call | tf_op jit(solution)/shard_map/reduce_grads/pallas_call | solution.py:324
  105.9 0.6 copy.15
  106.5 0.6 copy.14
  107.1 0.7 copy.19
  (2 shorter events, 0.0 us)
Async XLA Ops:
  2.2 1.0 copy-start
  3.1 0.9 copy-start.1
  47.5 0.7 copy-start.2

commit v3 on v0

v3 whole, which is shorter than its diff:
```python
import math

import jax
import jax.numpy as jnp
from jax import lax
from jax.experimental import pallas as pl
from jax.experimental.pallas import tpu as pltpu
from jax.sharding import PartitionSpec as P

MESH = pl.DeviceIdType.MESH
F32 = jnp.float32
BF16 = jnp.bfloat16
NX, NZ = 4, 16
NQ = NZ // 2
PEERS = 8
TOK = 8
GROUP = 16
DH = 128
TILES = 4
TR = PEERS * TOK * GROUP // TILES
CHUNKS = NX * 2 * PEERS
KEYS = CHUNKS * TOK
SCALE = DH ** -0.5
RATE = SCALE * math.log2(math.e)
Z_ORDER = (1, 7, 2, 6, 3, 5, 4)
X_ORDER = (1, 3, 2)
BACK = Z_ORDER[::-1] + (0,)


def place():
    blk = lax.axis_index("blk")
    head = lax.axis_index("head")
    z = (blk // 8) * 4 + head % 4
    return (blk // 2) % 4, head // 4, z, blk % 2


def device(x, y, z, c):
    return (((z // 4) * 4 + x) * 2 + c, y * 4 + z % 4)


def peer(x, z, c, n):
    return device(x, n // 2, (z // 2) * 2 + n % 2, c)


def dot(a, b):
    return lax.dot_general(a, b, (((1,), (0,)), ((), ())), preferred_element_type=F32)


def kernel(
    order_ref, q_ref, g_ref, kv_ref, dqh_ref, dkvh_ref,
    qa, ga, qt, gt, kvg, ks, vs, kt, pos, prob, dprob, tops, top, total, mixed, dk, dv, dqt, dqs,
    dkv, cx, xst, xr, zst, zr, fst,
    p_s, p_r, z_s, z_r, x_s, x_r, c_s, c_r, q_s, q_r, g_s, g_r,
    d_s, d_r, e_s, e_r, f_s, f_r, h_s, h_r, o_s, o_r, own,
):
    x, y, z, c = place()
    m = y * 2 + z % 2
    zq = z // 2
    other = device(x, y, z, 1 - c)
    sends = []

    def copy(src, dst, ss, rs, to):
        return pltpu.make_async_remote_copy(
            src_ref=src, dst_ref=dst, send_sem=ss, recv_sem=rs, device_id=to, device_id_type=MESH
        )

    def start(src, dst, ss, rs, to):
        one = copy(src, dst, ss, rs, to)
        one.start()
        sends.append(one)

    def arrived(dst, ss, rs):
        copy(dst, dst, ss, rs, other).wait_recv()

    barrier = pltpu.get_barrier_semaphore()
    to = [peer(x, z, c, (m + d) % PEERS) for d in range(1, PEERS)]
    to += [device(x, y, (z + 2 * d) % NZ, c) for d in range(1, NQ)]
    to += [device((x + d) % NX, y, z, c) for d in range(1, NX)]
    to += [other]
    for one in to:
        pl.semaphore_signal(barrier, inc=1, device_id=one, device_id_type=MESH)

    kv_own = pltpu.make_async_copy(kv_ref.at[m], kvg.at[zq, x, c, m], own.at[0])
    kv_own.start()
    q_own = pltpu.make_async_copy(q_ref.at[:, pl.ds(m * GROUP, GROUP), :], qa.at[m], own.at[1])
    g_own = pltpu.make_async_copy(g_ref.at[:, pl.ds(m * GROUP, GROUP), :], ga.at[m], own.at[2])
    q_own.start()
    g_own.start()

    step = lax.broadcasted_iota(jnp.int32, (TOK, DH), 0)

    def place_keys(d, carry):
        zk = (zq + NQ - d) % NQ
        for j in range(NX * 2):
            for h in range(2):
                first = order_ref[(zk // 2) * 16 + j * 2 + h] * 64 + (zk % 2) * 16
                for k in range(4):
                    at = (j * PEERS + h * 4 + k) * TOK
                    pos[d, at:at + TOK, :] = first + (k // 2) * 32 + (k % 2) * 8 + step
        return carry

    lax.fori_loop(0, NQ, place_keys, 0)
    top[...] = jnp.full_like(top, -1e30)
    total[...] = jnp.zeros_like(total)
    mixed[...] = jnp.zeros_like(mixed)
    dqt[...] = jnp.zeros_like(dqt)
    pl.semaphore_wait(barrier, len(to))

    for d in range(1, PEERS):
        n = (m + d) % PEERS
        start(kv_ref.at[n], kvg.at[zq, x, c, m], p_s.at[d], p_r.at[d], peer(x, z, c, n))
    kv_own.wait()
    for d in range(1, PEERS):
        arrived(kvg.at[zq, x, c, (m + PEERS - d) % PEERS], p_s.at[d], p_r.at[d])
    block = kvg.at[zq, x, c]
    for d in Z_ORDER:
        start(block, block, z_s.at[d], z_r.at[d], device(x, y, (z + 2 * d) % NZ, c))

    def share(d):
        block = kvg.at[(zq + NQ - d) % NQ, x, c]
        for e in X_ORDER:
            start(block, block, x_s.at[d, e], x_r.at[d, e], device((x + e) % NX, y, z, c))

    def swap(d):
        zk = (zq + NQ - d) % NQ
        for e in X_ORDER:
            arrived(kvg.at[zk, (x + NX - e) % NX, c], x_s.at[d, e], x_r.at[d, e])
        start(kvg.at[zk, :, c], kvg.at[zk, :, c], c_s.at[d], c_r.at[d], other)

    share(0)
    for d in range(1, PEERS):
        n = (m + d) % PEERS
        to = peer(x, z, c, n)
        start(q_ref.at[:, pl.ds(n * GROUP, GROUP), :], qa.at[m], q_s.at[d], q_r.at[d], to)
        start(g_ref.at[:, pl.ds(n * GROUP, GROUP), :], ga.at[m], g_s.at[d], g_r.at[d], to)

    lane = lax.broadcasted_iota(jnp.int32, (1, TR), 1)
    blk = (z // 4 * 4 + x) * 2 + c

    def take_queries():
        q_own.wait()
        g_own.wait()
        for d in range(1, PEERS):
            n = (m + PEERS - d) % PEERS
            arrived(qa.at[n], q_s.at[d], q_r.at[d])
            arrived(ga.at[n], g_s.at[d], g_r.at[d])
        for t in range(TILES):
            qt[t] = qa[2 * t:2 * t + 2].reshape(TR, DH).T
            gt[t] = ga[2 * t:2 * t + 2].reshape(TR, DH).T

    def score(d):
        zk = (zq + NQ - d) % NQ
        arrived(kvg.at[zk, :, 1 - c], c_s.at[d], c_r.at[d])
        both = kvg[zk].reshape(CHUNKS, 16, DH).astype(F32).reshape(CHUNKS, 2, TOK, DH)
        k = both[:, 0].reshape(KEYS, DH).astype(BF16)
        ks[...] = k
        kt[d] = k.T
        vs[...] = both[:, 1].reshape(KEYS, DH).astype(BF16)

        def tile(t, carry):
            limit = (
                order_ref[blk * 2 + t // 2] * 64 + (t % 2) * 32 + (z % 4 // 2) * 16
                + (lane // 128) * 8 + (lane // GROUP) % TOK
            )
            s = dot(ks[...], qt[t])
            at = pos[d]
            s = jnp.where(jnp.concatenate((at, at), axis=1) <= limit, s, -1e30)
            old = top[t]
            new = jnp.maximum(old, jnp.max(s, axis=0, keepdims=True))
            e = jnp.exp2((s - new) * RATE)
            prob[d, t] = e
            dp = dot(vs[...], gt[t])
            dprob[d, t] = dp
            fade = jnp.exp2((old - new) * RATE)
            total[t] = total[t] * fade + jnp.sum(e, axis=0, keepdims=True)
            mixed[t] = mixed[t] * fade + jnp.sum(e * dp, axis=0, keepdims=True)
            tops[d, t] = new
            top[t] = new
            return carry

        lax.fori_loop(0, TILES, tile, 0)

    visits = (0,) + Z_ORDER
    for k, d in enumerate(visits):
        if k:
            arrived(kvg.at[(zq + NQ - d) % NQ, x, c], z_s.at[d], z_r.at[d])
            share(d)
            swap(visits[k - 1])
        if k == 1:
            take_queries()
        if k >= 2:
            score(visits[k - 2])
    swap(visits[-1])
    score(visits[-2])
    score(visits[-1])
    total[...] = 1.0 / total[...]
    mixed[...] = mixed[...] * total[...]

    def grads(d):
        u = (NQ - d) % NQ
        dk[...] = jnp.zeros_like(dk)
        dv[...] = jnp.zeros_like(dv)

        def tile(t, carry):
            share_of = jnp.exp2((tops[u, t] - top[t]) * RATE) * total[t]
            p = prob[u, t] * share_of
            ds = (p * (dprob[u, t] - mixed[t])).astype(BF16)
            dv[...] += dot(p.astype(BF16), ga[pl.ds(2 * t, 2)].reshape(TR, DH))
            dk[...] += dot(ds, qa[pl.ds(2 * t, 2)].reshape(TR, DH))
            dqt[t] += dot(kt[u], ds)
            return carry

        lax.fori_loop(0, TILES, tile, 0)
        both = jnp.stack(((dk[...] * SCALE).reshape(CHUNKS, TOK, DH), dv[...].reshape(CHUNKS, TOK, DH)), axis=1)
        dkv[d] = both.reshape(NX, 2, PEERS, 16, DH).astype(BF16)
        start(dkv.at[d, :, 1 - c], cx.at[d], d_s.at[d], d_r.at[d], other)

    def along_x(d):
        arrived(cx.at[d], d_s.at[d], d_r.at[d])
        for e in X_ORDER:
            xd = (x + e) % NX
            xst[d, e] = (dkv[d, xd, c].astype(F32) + cx[d, xd].astype(F32)).astype(BF16)
            start(xst.at[d, e], xr.at[d, e], e_s.at[d, e], e_r.at[d, e], device(xd, y, z, c))

    def along_z(d):
        part = dkv[d, x, c].astype(F32) + cx[d, x].astype(F32)
        for e in X_ORDER:
            arrived(xr.at[d, e], e_s.at[d, e], e_r.at[d, e])
            part = part + xr[d, e].astype(F32)
        if d:
            zst[d] = part.astype(BF16)
            start(zst.at[d], zr.at[d], f_s.at[d], f_r.at[d], device(x, y, (z + 2 * d) % NZ, c))
        return part

    for k, d in enumerate(BACK):
        grads(d)
        if k >= 1:
            along_x(BACK[k - 1])
        if k >= 3:
            along_z(BACK[k - 3])
    along_x(BACK[-1])
    along_z(BACK[-3])
    for t in range(TILES):
        dqs[2 * t:2 * t + 2] = (dqt[t] * SCALE).T.astype(BF16).reshape(2, TOK, GROUP, DH)
    along_z(BACK[-2])
    dq_own = pltpu.make_async_copy(dqs.at[m], dqh_ref.at[:, pl.ds(m * GROUP, GROUP), :], own.at[3])
    dq_own.start()
    for d in range(1, PEERS):
        n = (m + d) % PEERS
        start(dqs.at[n], dqh_ref.at[:, pl.ds(m * GROUP, GROUP), :], o_s.at[d], o_r.at[d], peer(x, z, c, n))
    part = along_z(BACK[-1])
    for d in BACK[:-1]:
        arrived(zr.at[d], f_s.at[d], f_r.at[d])
        part = part + zr[d].astype(F32)
    fst[...] = part.astype(BF16)
    for d in range(1, PEERS):
        n = (m + d) % PEERS
        start(fst.at[n], dkvh_ref.at[m], h_s.at[d], h_r.at[d], peer(x, z, c, n))
    kv_home = pltpu.make_async_copy(fst.at[m], dkvh_ref.at[m], own.at[4])
    kv_home.start()
    dq_own.wait()
    kv_home.wait()
    for d in range(1, PEERS):
        n = (m + PEERS - d) % PEERS
        arrived(dqh_ref.at[:, pl.ds(n * GROUP, GROUP), :], o_s.at[d], o_r.at[d])
        arrived(dkvh_ref.at[n], h_s.at[d], h_r.at[d])
    for one in sends:
        one.wait_send()


def backward(order, q, g, kv):
    sem = pltpu.SemaphoreType.DMA
    hbm = pl.BlockSpec(memory_space=pl.ANY)
    vmem = pl.BlockSpec(memory_space=pltpu.VMEM)
    block = (PEERS, 16, DH)
    rows = (PEERS, TOK, GROUP, DH)
    stat = pltpu.VMEM((TILES, 1, TR), F32)
    one, two = sem((NQ,)), sem((NQ, NX))
    return pl.pallas_call(
        kernel,
        out_shape=(jax.ShapeDtypeStruct((TOK, PEERS * GROUP, DH), BF16), jax.ShapeDtypeStruct(block, BF16)),
        in_specs=[pl.BlockSpec(memory_space=pltpu.SMEM), hbm, hbm, hbm],
        out_specs=[vmem, vmem],
        scratch_shapes=[
            pltpu.VMEM(rows, BF16), pltpu.VMEM(rows, BF16),
            pltpu.VMEM((TILES, DH, TR), BF16), pltpu.VMEM((TILES, DH, TR), BF16),
            pltpu.VMEM((NQ, NX, 2) + block, BF16),
            pltpu.VMEM((KEYS, DH), BF16), pltpu.VMEM((KEYS, DH), BF16), pltpu.VMEM((NQ, DH, KEYS), BF16),
            pltpu.VMEM((NQ, KEYS, DH), jnp.int32),
            pltpu.VMEM((NQ, TILES, KEYS, TR), F32), pltpu.VMEM((NQ, TILES, KEYS, TR), F32),
            pltpu.VMEM((NQ, TILES, 1, TR), F32), stat, stat, stat,
            pltpu.VMEM((KEYS, DH), F32), pltpu.VMEM((KEYS, DH), F32),
            pltpu.VMEM((TILES, DH, TR), F32), pltpu.VMEM(rows, BF16),
            pltpu.VMEM((NQ, NX, 2) + block, BF16), pltpu.VMEM((NQ, NX) + block, BF16),
            pltpu.VMEM((NQ, NX) + block, BF16), pltpu.VMEM((NQ, NX) + block, BF16),
            pltpu.VMEM((NQ,) + block, BF16), pltpu.VMEM((NQ,) + block, BF16), pltpu.VMEM(block, BF16),
            one, one, one, one, two, two, one, one, one, one, one, one,
            one, one, two, two, one, one, one, one, one, one, sem((5,)),
        ],
        compiler_params=pltpu.CompilerParams(collective_id=0, has_side_effects=True, vmem_limit_bytes=58 << 20),
        name="attention_backward",
    )(order, q, g, kv)


def on_device(query, key, value, out_grad, block_order):
    kv = jnp.concatenate((jnp.transpose(key, (1, 0, 2)), jnp.transpose(value, (1, 0, 2))), axis=1)
    dq_home, dkv_home = backward(block_order, query, out_grad, kv)
    grads = jnp.transpose(dkv_home, (1, 0, 2))
    return dq_home, grads[:TOK], grads[TOK:]


def solution(mesh):
    rows = P(("blk", "head"), None, None)
    return jax.shard_map(
        on_device, mesh=mesh, in_specs=(rows,) * 4 + (P(),), out_specs=(rows,) * 3, check_vma=False
    )
```

time: 501 us -> 96.6 us (0.19)
  waiting for transfers between devices: 376 us -> 0 us
  Pallas kernels: 0 us -> 90.6 us
  matrix products: 42.7 us -> 0 us
  starting transfers between devices: 28.4 us -> 0 us
  local copies, waits for them, and re-layouts: 23.1 us -> 4.37 us
  between operations: 16.7 us -> 0.64 us
  other arithmetic: 9.68 us -> 0.62 us
    reduce_scatter x2 -> x0, waiting for transfers between devices: 240 us -> none  [the longest x1 121 us: on_device(): lax.psum_scatter(dv_term, 'blk', scatter_dimension=0, tiled=True)]
    all_gather x2 -> x0, waiting for transfers between devices: 110 us -> none  [the longest x1 59.5 us: on_device(): lax.all_gather(v_local, 'blk', axis=0, tiled=True)]
    pallas_call x0 -> x1, Pallas kernels: none -> 90.6 us  [backward(): pl.pallas_call(kernel, out_shape=(jax.ShapeDtypeStruct((TOK, PEERS * GROU...]
    dot_general x42 -> x0, matrix products: 42.7 us -> none  [the longest x12 11.5 us: scored(): jnp.einsum('qkgd,tkd->kgqt', queries, key_blk, preferred_element_type=jnp...]
    all_to_all x6 -> x0, starting transfers between devices: 28.2 us -> none  [the longest x1 9.19 us: on_device(): lax.all_to_all(key_rep, 'head', split_axis=1, concat_axis=0, tiled=True)]
    all_to_all x6 -> x0, waiting for transfers between devices: 26.1 us -> none  [the longest x1 6.23 us: on_device(): lax.all_to_all(key_mine.astype(jnp.bfloat16), 'head', split_axis=0, conca...]
    gather x4 -> x0, local copies, waits for them, and re-layouts: 9.54 us -> none  [the longest x1 3.62 us: on_device(): dv_term.reshape(piece_count, piece_len, local_kv, head_width)[block_order]]
  transfers between devices with their start and end apart: 10 -> 0, of which waited for: 9 -> 0; matrix products, arithmetic and copies ran while one was open for 4% -> 0% of each run, Pallas kernels for 0% -> 0%
where the time goes in v3:
time: 96.6 us; the launch traced here: 96.3 us
  Pallas kernels  90.6 us (94%)
  local copies, waits for them, and re-layouts  4.37 us (5%)
    pallas_call x1, Pallas kernels, backward(): pl.pallas_call(kernel, out_shape=(jax.ShapeDtypeStruct((TOK, PEERS * GROU...  90.6 us
    unnamed x3, local copies, waits for them, and re-layouts  2.89 us

profile of v3, /device:TPU:1, one launch (start us, length us, event | category | flops | bytes accessed | tf_op | source)
XLA Modules:
  0.0 96.3 jit_solution(17462084475643076069)
XLA Ops:
  0.6 0.7 copy_bitcast_fusion
  1.4 0.6 pad_maximum_fusion.kv_ref
  2.0 90.6 %attention_backward.1 = (bf16[8,128,128]{2,1,0:T(8,128)(2,1)}, bf16[8,16,128]{2,1,0:T(8,128)(2,1)}) custom-call(s32[64]{0:T(128)} %order_ref.1, bf16[8,128,128]{2,1,0:T(8,128)(2,1)} %q_ref.1, bf16[8,128,128]{2,1,0:T(8,128)(2,1)} %g_ref.1, bf16[8,16,128]{2,1,0:T(8,128)(2,1)} %pad_maximum_fusion.kv_ref), custom_call_target="tpu_custom_call" | custom-call | tf_op jit(solution)/shard_map/attention_backward/pallas_call | solution.py:279
  92.6 0.7 fusion
  93.4 0.6 copy.11
  94.0 0.6 copy.10
  94.6 1.7 %copy.15 = bf16[8,128,128]{2,1,0:T(8,128)(2,1)} copy(bf16[8,128,128]{2,1,0:T(8,128)(2,1)} %get-tuple-element.17) | data formatting | bytes 524288

commit v4 on v3

v4 whole, which is shorter than its diff:
```python
import math

import jax
import jax.numpy as jnp
from jax import lax
from jax.experimental import pallas as pl
from jax.experimental.pallas import tpu as pltpu
from jax.sharding import PartitionSpec as P

MESH = pl.DeviceIdType.MESH
F32 = jnp.float32
BF16 = jnp.bfloat16
NX, NY, NZ = 4, 4, 16
PLANE = NX * NY
HEADS = 8
TOK = 8
GROUP = 16
DH = 128
TILES = 4
TR = HEADS * TOK * GROUP // TILES
CHUNKS = 2 * NZ
KEYS = CHUNKS * TOK
SCALE = DH ** -0.5
RATE = SCALE * math.log2(math.e)
PAIRS = ((1, 3), (4, 12), (5, 15), (7, 13), (2, 8), (6, 14), (9, 11), (0, 10))
UNITS = len(PAIRS)
NEAR = tuple(d for pair in PAIRS for d in pair if d)


def opposite(d):
    return (NX - d // NY) % NX * NY + (NY - d % NY) % NY


def place():
    blk = lax.axis_index("blk")
    head = lax.axis_index("head")
    z = (blk // 8) * 4 + head % 4
    return (blk // 2) % 4, head // 4, z, blk % 2


def device(x, y, z, c):
    return (((z // 4) * 4 + x) * 2 + c, y * 4 + z % 4)


def turn(o, z):
    return 8 * ((o + 3) // 8) + 8 * (z % 2) * (o // 4 - (o + 3) // 8)


def given_to(o, z):
    return (z + o + turn(o, z)) % NZ


def got_from(o, z):
    return (z + NZ - o + turn(o, z)) % NZ


def dot(a, b):
    return lax.dot_general(a, b, (((1,), (0,)), ((), ())), preferred_element_type=F32)


def kernel(
    order_ref, q_ref, k_ref, v_ref, g_ref, dqh_ref, dkh_ref, dvh_ref,
    kin, vin, kv, qa, ga, qt, gt, kvg, ks, vs, kt, pos, prob, dprob, tops, top, total, mixed, dk, dv, dqt, dqs,
    dkv, cx, pst, pr, fst, fin,
    k_s, k_r, p_s, p_r, c_s, c_r, q_s, q_r, g_s, g_r, d_s, d_r, e_s, e_r, f_s, f_r, o_s, o_r, own,
):
    x, y, z, c = place()
    i = x * NY + y
    head = z % HEADS
    other = device(x, y, z, 1 - c)
    sends = []

    def copy(src, dst, ss, rs, to):
        return pltpu.make_async_remote_copy(
            src_ref=src, dst_ref=dst, send_sem=ss, recv_sem=rs, device_id=to, device_id_type=MESH
        )

    def start(src, dst, ss, rs, to):
        one = copy(src, dst, ss, rs, to)
        one.start()
        sends.append(one)

    def arrived(dst, ss, rs):
        copy(dst, dst, ss, rs, other).wait_recv()

    def local(src, dst, at):
        one = pltpu.make_async_copy(src, dst, own.at[at])
        one.start()
        return one

    def away(d):
        return device((x + d // NY) % NX, (y + d % NY) % NY, z, c)

    def source(d):
        return (x + NX - d // NY) % NX * NY + (y + NY - d % NY) % NY

    barrier = pltpu.get_barrier_semaphore()
    to = [device(x, y, (z + d) % NZ, c) for d in range(1, NZ)]
    to += [away(d) for d in range(1, PLANE)]
    to += [other]
    for one in to:
        pl.semaphore_signal(barrier, inc=1, device_id=one, device_id_type=MESH)

    k_in = local(k_ref, kin, 0)
    v_in = local(v_ref, vin, 1)
    q_own = local(q_ref.at[:, pl.ds(head * GROUP, GROUP), :], qa.at[0], 2)
    g_own = local(g_ref.at[:, pl.ds(head * GROUP, GROUP), :], ga.at[0], 3)
    k_in.wait()
    v_in.wait()
    kv[...] = jnp.concatenate(
        (jnp.swapaxes(kin[...].astype(F32), 0, 1), jnp.swapaxes(vin[...].astype(F32), 0, 1)), axis=1
    ).astype(BF16)
    kv_own = local(kv.at[head], kvg.at[i, c, z], 4)

    step = lax.broadcasted_iota(jnp.int32, (TOK, DH), 0)

    def place_keys(d, carry):
        xs = (x + NX - d // NY) % NX
        ys = (y + NY - d % NY) % NY
        for cc in range(2):
            for zz in range(NZ):
                first = order_ref[(zz // 4) * 16 + xs * 4 + cc * 2 + ys // 2] * 64 + (ys % 2) * 32 + (zz % 4) * 8
                at = (cc * NZ + zz) * TOK
                pos[d, at:at + TOK, :] = first + step
        return carry

    lax.fori_loop(0, PLANE, place_keys, 0)
    top[...] = jnp.full_like(top, -1e30)
    total[...] = jnp.zeros_like(total)
    mixed[...] = jnp.zeros_like(mixed)
    dqt[...] = jnp.zeros_like(dqt)
    pl.semaphore_wait(barrier, len(to))

    for d in range(1, NZ):
        zd = (z + d) % NZ
        start(kv.at[zd % HEADS], kvg.at[i, c, z], k_s.at[d], k_r.at[d], device(x, y, zd, c))
    kv_own.wait()
    for d in range(1, NZ):
        arrived(kvg.at[i, c, (z + NZ - d) % NZ], k_s.at[d], k_r.at[d])
    for d in NEAR:
        start(kvg.at[i, c], kvg.at[i, c], p_s.at[d], p_r.at[d], away(d))
    start(kvg.at[i, c], kvg.at[i, c], c_s.at[0], c_r.at[0], other)
    for o in range(1, HEADS):
        zd = given_to(o, z)
        rows = pl.ds(zd % HEADS * GROUP, GROUP)
        start(q_ref.at[:, rows, :], qa.at[o], q_s.at[o], q_r.at[o], device(x, y, zd, c))
        start(g_ref.at[:, rows, :], ga.at[o], g_s.at[o], g_r.at[o], device(x, y, zd, c))

    lane = lax.broadcasted_iota(jnp.int32, (1, TR), 1)

    def take_queries():
        q_own.wait()
        g_own.wait()
        for o in range(1, HEADS):
            arrived(qa.at[o], q_s.at[o], q_r.at[o])
            arrived(ga.at[o], g_s.at[o], g_r.at[o])
        for t in range(TILES):
            qt[t] = qa[2 * t:2 * t + 2].reshape(TR, DH).T
            gt[t] = ga[2 * t:2 * t + 2].reshape(TR, DH).T

    def swap(d):
        if d:
            p = source(d)
            arrived(kvg.at[p, c], p_s.at[d], p_r.at[d])
            start(kvg.at[p, c], kvg.at[p, c], c_s.at[d], c_r.at[d], other)

    def score(u):
        for j, d in enumerate(PAIRS[u]):
            p = source(d)
            arrived(kvg.at[p, 1 - c], c_s.at[d], c_r.at[d])
            both = kvg[p].reshape(CHUNKS, 16, DH).astype(F32).reshape(CHUNKS, 2, TOK, DH)
            k = both[:, 0].reshape(KEYS, DH).astype(BF16)
            ks[j * KEYS:(j + 1) * KEYS, :] = k
            kt[u, :, j * KEYS:(j + 1) * KEYS] = k.T
            vs[j * KEYS:(j + 1) * KEYS, :] = both[:, 1].reshape(KEYS, DH).astype(BF16)

        def tile(t, carry):
            limit = (lane // GROUP) % TOK + (y % 2) * 32
            for j in range(2):
                zs = got_from(2 * t + j, z)
                first = order_ref[(zs // 4) * 16 + x * 4 + c * 2 + y // 2] * 64 + (zs % 4) * 8
                limit = limit + jnp.where(lane // DH == j, first, 0)
            s = dot(ks[...], qt[t])
            at = jnp.concatenate((pos[PAIRS[u][0]], pos[PAIRS[u][1]]), axis=0)
            s = jnp.where(jnp.concatenate((at, at), axis=1) <= limit, s, -1e30)
            old = top[t]
            new = jnp.maximum(old, jnp.max(s, axis=0, keepdims=True))
            e = jnp.exp2((s - new) * RATE)
            prob[u, t] = e
            dp = dot(vs[...], gt[t])
            dprob[u, t] = dp
            fade = jnp.exp2((old - new) * RATE)
            total[t] = total[t] * fade + jnp.sum(e, axis=0, keepdims=True)
            mixed[t] = mixed[t] * fade + jnp.sum(e * dp, axis=0, keepdims=True)
            tops[u, t] = new
            top[t] = new
            return carry

        lax.fori_loop(0, TILES, tile, 0)

    for u in range(UNITS):
        for d in PAIRS[u]:
            swap(d)
        if u == 1:
            take_queries()
        if u >= 1:
            score(u - 1)
    score(UNITS - 1)
    total[...] = 1.0 / total[...]
    mixed[...] = mixed[...] * total[...]

    def grads(u):
        dk[...] = jnp.zeros_like(dk)
        dv[...] = jnp.zeros_like(dv)

        def tile(t, carry):
            share_of = jnp.exp2((tops[u, t] - top[t]) * RATE) * total[t]
            p = prob[u, t] * share_of
            ds = (p * (dprob[u, t] - mixed[t])).astype(BF16)
            dv[...] += dot(p.astype(BF16), ga[pl.ds(2 * t, 2)].reshape(TR, DH))
            dk[...] += dot(ds, qa[pl.ds(2 * t, 2)].reshape(TR, DH))
            dqt[t] += dot(kt[u], ds)
            return carry

        lax.fori_loop(0, TILES, tile, 0)
        for j, d in enumerate(PAIRS[u]):
            rows = slice(j * KEYS, (j + 1) * KEYS)
            both = jnp.stack(((dk[rows, :] * SCALE).reshape(CHUNKS, TOK, DH), dv[rows, :].reshape(CHUNKS, TOK, DH)), axis=1)
            dkv[d] = both.reshape(2, NZ, 16, DH).astype(BF16)
            start(dkv.at[d, 1 - c], cx.at[d], d_s.at[d], d_r.at[d], other)

    def along(u):
        for d in PAIRS[u]:
            arrived(cx.at[d], d_s.at[d], d_r.at[d])
            if d:
                back = opposite(d)
                pst[d] = (dkv[d, c].astype(F32) + cx[d].astype(F32)).astype(BF16)
                start(pst.at[d], pr.at[back], e_s.at[back], e_r.at[back], away(back))

    late = tuple(reversed(range(UNITS)))
    for k, u in enumerate(late):
        grads(u)
        if k:
            along(late[k - 1])
    along(late[-1])
    for t in range(TILES):
        dqs[2 * t:2 * t + 2] = (dqt[t] * SCALE).T.astype(BF16).reshape(2, TOK, GROUP, DH)
    rows = pl.ds(head * GROUP, GROUP)
    dq_own = local(dqs.at[0], dqh_ref.at[:, rows, :], 2)
    for o in range(1, HEADS):
        start(dqs.at[o], dqh_ref.at[:, rows, :], o_s.at[o], o_r.at[o], device(x, y, got_from(o, z), c))
    part = dkv[0, c].astype(F32) + cx[0].astype(F32)
    for u in late:
        for d in PAIRS[u]:
            if d:
                arrived(pr.at[d], e_s.at[d], e_r.at[d])
                part = part + pr[d].astype(F32)
    fst[...] = part.astype(BF16)
    for d in range(1, NZ):
        zd = (z + d) % NZ
        start(fst.at[zd], fin.at[z], f_s.at[d], f_r.at[d], device(x, y, zd, c))
    kv_home = local(fst.at[z], fin.at[z], 4)
    kv_home.wait()
    for d in range(1, NZ):
        arrived(fin.at[(z + NZ - d) % NZ], f_s.at[d], f_r.at[d])
    home = fin[:HEADS].astype(F32) + fin[HEADS:].astype(F32)
    dkh_ref[...] = jnp.swapaxes(home[:, :TOK], 0, 1).astype(BF16)
    dvh_ref[...] = jnp.swapaxes(home[:, TOK:], 0, 1).astype(BF16)
    dq_own.wait()
    for o in range(1, HEADS):
        arrived(dqh_ref.at[:, pl.ds(given_to(o, z) % HEADS * GROUP, GROUP), :], o_s.at[o], o_r.at[o])
    for one in sends:
        one.wait_send()


def backward(order, query, key, value, out_grad):
    sem = pltpu.SemaphoreType.DMA
    hbm = pl.BlockSpec(memory_space=pl.ANY)
    vmem = pl.BlockSpec(memory_space=pltpu.VMEM)
    block = (NZ, 16, DH)
    rows = (HEADS, TOK, GROUP, DH)
    home = (TOK, HEADS, DH)
    stat = pltpu.VMEM((TILES, 1, TR), F32)
    eight, many = sem((HEADS,)), sem((NZ,))
    return pl.pallas_call(
        kernel,
        out_shape=(
            jax.ShapeDtypeStruct((TOK, HEADS * GROUP, DH), BF16),
            jax.ShapeDtypeStruct(home, BF16),
            jax.ShapeDtypeStruct(home, BF16),
        ),
        in_specs=[pl.BlockSpec(memory_space=pltpu.SMEM), hbm, hbm, hbm, hbm],
        out_specs=[vmem, vmem, vmem],
        scratch_shapes=[
            pltpu.VMEM(home, BF16), pltpu.VMEM(home, BF16), pltpu.VMEM((HEADS, 16, DH), BF16),
            pltpu.VMEM(rows, BF16), pltpu.VMEM(rows, BF16),
            pltpu.VMEM((TILES, DH, TR), BF16), pltpu.VMEM((TILES, DH, TR), BF16),
            pltpu.VMEM((PLANE, 2) + block, BF16),
            pltpu.VMEM((2 * KEYS, DH), BF16), pltpu.VMEM((2 * KEYS, DH), BF16), pltpu.VMEM((UNITS, DH, 2 * KEYS), BF16),
            pltpu.VMEM((PLANE, KEYS, DH), jnp.int32),
            pltpu.VMEM((UNITS, TILES, 2 * KEYS, TR), F32), pltpu.VMEM((UNITS, TILES, 2 * KEYS, TR), F32),
            pltpu.VMEM((UNITS, TILES, 1, TR), F32), stat, stat, stat,
            pltpu.VMEM((2 * KEYS, DH), F32), pltpu.VMEM((2 * KEYS, DH), F32),
            pltpu.VMEM((TILES, DH, TR), F32), pltpu.VMEM(rows, BF16),
            pltpu.VMEM((PLANE, 2) + block, BF16), pltpu.VMEM((PLANE,) + block, BF16),
            pltpu.VMEM((PLANE,) + block, BF16), pltpu.VMEM((PLANE,) + block, BF16),
            pltpu.VMEM(block, BF16), pltpu.VMEM(block, BF16),
            many, many, many, many, many, many, eight, eight, eight, eight,
            many, many, many, many, many, many, eight, eight, sem((5,)),
        ],
        compiler_params=pltpu.CompilerParams(collective_id=0, has_side_effects=True, vmem_limit_bytes=58 << 20),
        name="attention_backward",
    )(order, query, key, value, out_grad)


def on_device(query, key, value, out_grad, block_order):
    return backward(block_order, query, key, value, out_grad)


def solution(mesh):
    rows = P(("blk", "head"), None, None)
    return jax.shard_map(
        on_device, mesh=mesh, in_specs=(rows,) * 4 + (P(),), out_specs=(rows,) * 3, check_vma=False
    )
```

time: 96.6 us -> 87.5 us (0.906)
  Pallas kernels: 90.6 us -> 83.5 us
  local copies, waits for them, and re-layouts: 4.37 us -> 3.01 us
    pallas_call x1, Pallas kernels: 90.6 us -> 83.5 us  [backward(): pl.pallas_call(kernel, out_shape=(jax.ShapeDtypeStruct((TOK, HEADS * GROU...]
    unnamed x3 -> x7, local copies, waits for them, and re-layouts: 2.89 us -> 3.01 us
where the time goes in v4:
time: 87.5 us; the launch traced here: 87.2 us
  Pallas kernels  83.5 us (95%)
  local copies, waits for them, and re-layouts  3.01 us (3%)
    pallas_call x1, Pallas kernels, backward(): pl.pallas_call(kernel, out_shape=(jax.ShapeDtypeStruct((TOK, HEADS * GROU...  83.5 us
    unnamed x7, local copies, waits for them, and re-layouts  3.01 us

profile of v4, /device:TPU:1, one launch (start us, length us, event | category | flops | bytes accessed | tf_op | source)
XLA Modules:
  0.0 87.2 jit_solution(5921767559709622376)
XLA Ops:
  0.6 83.5 %attention_backward.1 = (bf16[8,128,128]{2,1,0:T(8,128)(2,1)}, bf16[8,8,128]{2,1,0:T(8,128)(2,1)}, bf16[8,8,128]{2,1,0:T(8,128)(2,1)}) custom-call(s32[64]{0:T(128)} %order_ref.1, bf16[8,128,128]{2,1,0:T(8,128)(2,1)} %q_ref.1, bf16[8,8,128]{2,1,0:T(8,128)(2,1)} %k_ref.1, bf16[8,8,128]{2,1,0:T(8,128)(2,1)} %v_ref.1, bf16[8,128,128]{2,1,0:T(8,128)(2,1)} %g_ref.1), custom_call_target="tpu_custom_call" | custom-call | tf_op jit(solution)/shard_map/attention_backward/pallas_call | solution.py:285
  84.1 0.0 copy-start.1
  84.2 1.7 %copy.11 = bf16[8,128,128]{2,1,0:T(8,128)(2,1)} copy(bf16[8,128,128]{2,1,0:T(8,128)(2,1)} %get-tuple-element.6) | data formatting | bytes 524288
  85.8 0.0 copy-done.1
  85.8 0.0 copy-start
  85.8 0.6 copy.12
  86.4 0.1 copy-done
  86.6 0.6 copy.13
Async XLA Ops:
  84.1 1.7 %copy-start.1 = (bf16[8,8,128]{2,1,0:T(8,128)(2,1)S(1)}, bf16[8,8,128]{2,1,0:T(8,128)(2,1)}, u32[]{:S(2)}) copy-start(bf16[8,8,128]{2,1,0:T(8,128)(2,1)} %get-tuple-element.7) | copy-start | bytes 49156
  85.8 0.7 copy-start

commit v5 on v4

--- a/solution.py
+++ b/solution.py
@@ -134,17 +134,22 @@
     for d in range(1, NZ):
         zd = (z + d) % NZ
         start(kv.at[zd % HEADS], kvg.at[i, c, z], k_s.at[d], k_r.at[d], device(x, y, zd, c))
-    kv_own.wait()
-    for d in range(1, NZ):
-        arrived(kvg.at[i, c, (z + NZ - d) % NZ], k_s.at[d], k_r.at[d])
-    for d in NEAR:
-        start(kvg.at[i, c], kvg.at[i, c], p_s.at[d], p_r.at[d], away(d))
-    start(kvg.at[i, c], kvg.at[i, c], c_s.at[0], c_r.at[0], other)
     for o in range(1, HEADS):
         zd = given_to(o, z)
         rows = pl.ds(zd % HEADS * GROUP, GROUP)
         start(q_ref.at[:, rows, :], qa.at[o], q_s.at[o], q_r.at[o], device(x, y, zd, c))
         start(g_ref.at[:, rows, :], ga.at[o], g_s.at[o], g_r.at[o], device(x, y, zd, c))
+    kv_own.wait()
+    for d in range(1, NZ):
+        arrived(kvg.at[i, c, (z + NZ - d) % NZ], k_s.at[d], k_r.at[d])
+    def spread(u):
+        for d in PAIRS[u]:
+            if d:
+                start(kvg.at[i, c], kvg.at[i, c], p_s.at[d], p_r.at[d], away(d))
+
+    for u in range(3):
+        spread(u)
+    start(kvg.at[i, c], kvg.at[i, c], c_s.at[0], c_r.at[0], other)
 
     lane = lax.broadcasted_iota(jnp.int32, (1, TR), 1)
 
@@ -196,11 +201,13 @@
             top[t] = new
             return carry
 
-        lax.fori_loop(0, TILES, tile, 0)
+        lax.fori_loop(0, TILES, tile, 0, unroll=4)
 
     for u in range(UNITS):
         for d in PAIRS[u]:
             swap(d)
+        if u + 3 < UNITS:
+            spread(u + 3)
         if u == 1:
             take_queries()
         if u >= 1:
@@ -222,7 +229,7 @@
             dqt[t] += dot(kt[u], ds)
             return carry
 
-        lax.fori_loop(0, TILES, tile, 0)
+        lax.fori_loop(0, TILES, tile, 0, unroll=4)
         for j, d in enumerate(PAIRS[u]):
             rows = slice(j * KEYS, (j + 1) * KEYS)
             both = jnp.stack(((dk[rows, :] * SCALE).reshape(CHUNKS, TOK, DH), dv[rows, :].reshape(CHUNKS, TOK, DH)), axis=1)

time: 87.5 us -> 79.9 us (0.913)
  Pallas kernels: 83.5 us -> 75.3 us
    pallas_call x1, Pallas kernels: 83.5 us -> 75.3 us  [backward(): pl.pallas_call(kernel, out_shape=(jax.ShapeDtypeStruct((TOK, HEADS * GROU...]
where the time goes in v5:
time: 79.9 us; the launch traced here: 79 us
  Pallas kernels  75.3 us (94%)
  local copies, waits for them, and re-layouts  3.01 us (4%)
    pallas_call x1, Pallas kernels, backward(): pl.pallas_call(kernel, out_shape=(jax.ShapeDtypeStruct((TOK, HEADS * GROU...  75.3 us
    unnamed x7, local copies, waits for them, and re-layouts  3.01 us

profile of v5, /device:TPU:1, one launch (start us, length us, event | category | flops | bytes accessed | tf_op | source)
XLA Modules:
  0.0 79.0 jit_solution(6520893374208858129)
XLA Ops:
  0.6 75.3 %attention_backward.1 = (bf16[8,128,128]{2,1,0:T(8,128)(2,1)}, bf16[8,8,128]{2,1,0:T(8,128)(2,1)}, bf16[8,8,128]{2,1,0:T(8,128)(2,1)}) custom-call(s32[64]{0:T(128)} %order_ref.1, bf16[8,128,128]{2,1,0:T(8,128)(2,1)} %q_ref.1, bf16[8,8,128]{2,1,0:T(8,128)(2,1)} %k_ref.1, bf16[8,8,128]{2,1,0:T(8,128)(2,1)} %v_ref.1, bf16[8,128,128]{2,1,0:T(8,128)(2,1)} %g_ref.1), custom_call_target="tpu_custom_call" | custom-call | tf_op jit(solution)/shard_map/attention_backward/pallas_call | solution.py:292
  76.0 0.0 copy-start.1
  76.0 1.7 %copy.11 = bf16[8,128,128]{2,1,0:T(8,128)(2,1)} copy(bf16[8,128,128]{2,1,0:T(8,128)(2,1)} %get-tuple-element.6) | data formatting | bytes 524288
  77.7 0.0 copy-done.1
  77.7 0.0 copy-start
  77.7 0.6 copy.12
  78.3 0.1 copy-done
  78.4 0.6 copy.13
Async XLA Ops:
  76.0 1.7 %copy-start.1 = (bf16[8,8,128]{2,1,0:T(8,128)(2,1)S(1)}, bf16[8,8,128]{2,1,0:T(8,128)(2,1)}, u32[]{:S(2)}) copy-start(bf16[8,8,128]{2,1,0:T(8,128)(2,1)} %get-tuple-element.7) | copy-start | bytes 49156
  77.7 0.7 copy-start

commit v6 on v4

--- a/solution.py
+++ b/solution.py
@@ -24,6 +24,9 @@
 RATE = SCALE * math.log2(math.e)
 PAIRS = ((1, 3), (4, 12), (5, 15), (7, 13), (2, 8), (6, 14), (9, 11), (0, 10))
 UNITS = len(PAIRS)
+HERE = 4
+HALF = NZ // 2
+OUTWARD = (1, 15, 2, 14, 3, 13, 4, 12, 5, 11, 6, 10, 7, 9, 8)
 NEAR = tuple(d for pair in PAIRS for d in pair if d)
 
 
@@ -110,7 +113,18 @@
     kv[...] = jnp.concatenate(
         (jnp.swapaxes(kin[...].astype(F32), 0, 1), jnp.swapaxes(vin[...].astype(F32), 0, 1)), axis=1
     ).astype(BF16)
-    kv_own = local(kv.at[head], kvg.at[i, c, z], 4)
+    kv_own = local(kv.at[head], kvg.at[i, c, HERE], 4)
+
+    pl.semaphore_wait(barrier, len(to))
+
+    for d in OUTWARD:
+        zd = (z + d) % NZ
+        start(kv.at[zd % HEADS], kvg.at[i, c, (HERE - d) % NZ], k_s.at[d], k_r.at[d], device(x, y, zd, c))
+    for o in range(1, HEADS):
+        zd = given_to(o, z)
+        rows = pl.ds(zd % HEADS * GROUP, GROUP)
+        start(q_ref.at[:, rows, :], qa.at[o], q_s.at[o], q_r.at[o], device(x, y, zd, c))
+        start(g_ref.at[:, rows, :], ga.at[o], g_s.at[o], g_r.at[o], device(x, y, zd, c))
 
     step = lax.broadcasted_iota(jnp.int32, (TOK, DH), 0)
 
@@ -119,7 +133,8 @@
         ys = (y + NY - d % NY) % NY
         for cc in range(2):
             for zz in range(NZ):
-                first = order_ref[(zz // 4) * 16 + xs * 4 + cc * 2 + ys // 2] * 64 + (ys % 2) * 32 + (zz % 4) * 8
+                zs = (z + NZ + zz - HERE) % NZ
+                first = order_ref[(zs // 4) * 16 + xs * 4 + cc * 2 + ys // 2] * 64 + (ys % 2) * 32 + (zs % 4) * 8
                 at = (cc * NZ + zz) * TOK
                 pos[d, at:at + TOK, :] = first + step
         return carry
@@ -129,22 +144,16 @@
     total[...] = jnp.zeros_like(total)
     mixed[...] = jnp.zeros_like(mixed)
     dqt[...] = jnp.zeros_like(dqt)
-    pl.semaphore_wait(barrier, len(to))
-
-    for d in range(1, NZ):
-        zd = (z + d) % NZ
-        start(kv.at[zd % HEADS], kvg.at[i, c, z], k_s.at[d], k_r.at[d], device(x, y, zd, c))
+
     kv_own.wait()
-    for d in range(1, NZ):
-        arrived(kvg.at[i, c, (z + NZ - d) % NZ], k_s.at[d], k_r.at[d])
-    for d in NEAR:
-        start(kvg.at[i, c], kvg.at[i, c], p_s.at[d], p_r.at[d], away(d))
+    for part, slots in enumerate((pl.ds(0, HALF), pl.ds(HALF, HALF))):
+        for d in OUTWARD:
+            if (HERE - d) % NZ // HALF == part:
+                arrived(kvg.at[i, c, (HERE - d) % NZ], k_s.at[d], k_r.at[d])
+        for d in NEAR:
+            block = kvg.at[i, c, slots]
+            start(block, block, p_s.at[part, d], p_r.at[part, d], away(d))
     start(kvg.at[i, c], kvg.at[i, c], c_s.at[0], c_r.at[0], other)
-    for o in range(1, HEADS):
-        zd = given_to(o, z)
-        rows = pl.ds(zd % HEADS * GROUP, GROUP)
-        start(q_ref.at[:, rows, :], qa.at[o], q_s.at[o], q_r.at[o], device(x, y, zd, c))
-        start(g_ref.at[:, rows, :], ga.at[o], g_s.at[o], g_r.at[o], device(x, y, zd, c))
 
     lane = lax.broadcasted_iota(jnp.int32, (1, TR), 1)
 
@@ -161,7 +170,8 @@
     def swap(d):
         if d:
             p = source(d)
-            arrived(kvg.at[p, c], p_s.at[d], p_r.at[d])
+            for part in range(2):
+                arrived(kvg.at[p, c, pl.ds(part * HALF, HALF)], p_s.at[part, d], p_r.at[part, d])
             start(kvg.at[p, c], kvg.at[p, c], c_s.at[d], c_r.at[d], other)
 
     def score(u):
@@ -196,7 +206,7 @@
             top[t] = new
             return carry
 
-        lax.fori_loop(0, TILES, tile, 0)
+        lax.fori_loop(0, TILES, tile, 0, unroll=4)
 
     for u in range(UNITS):
         for d in PAIRS[u]:
@@ -222,7 +232,7 @@
             dqt[t] += dot(kt[u], ds)
             return carry
 
-        lax.fori_loop(0, TILES, tile, 0)
+        lax.fori_loop(0, TILES, tile, 0, unroll=4)
         for j, d in enumerate(PAIRS[u]):
             rows = slice(j * KEYS, (j + 1) * KEYS)
             both = jnp.stack(((dk[rows, :] * SCALE).reshape(CHUNKS, TOK, DH), dv[rows, :].reshape(CHUNKS, TOK, DH)), axis=1)
@@ -256,10 +266,9 @@
                 arrived(pr.at[d], e_s.at[d], e_r.at[d])
                 part = part + pr[d].astype(F32)
     fst[...] = part.astype(BF16)
-    for d in range(1, NZ):
-        zd = (z + d) % NZ
-        start(fst.at[zd], fin.at[z], f_s.at[d], f_r.at[d], device(x, y, zd, c))
-    kv_home = local(fst.at[z], fin.at[z], 4)
+    for d in reversed(OUTWARD):
+        start(fst.at[(HERE + d) % NZ], fin.at[z], f_s.at[d], f_r.at[d], device(x, y, (z + d) % NZ, c))
+    kv_home = local(fst.at[HERE], fin.at[z], 4)
     kv_home.wait()
     for d in range(1, NZ):
         arrived(fin.at[(z + NZ - d) % NZ], f_s.at[d], f_r.at[d])
@@ -281,7 +290,7 @@
     rows = (HEADS, TOK, GROUP, DH)
     home = (TOK, HEADS, DH)
     stat = pltpu.VMEM((TILES, 1, TR), F32)
-    eight, many = sem((HEADS,)), sem((NZ,))
+    eight, many, both = sem((HEADS,)), sem((NZ,)), sem((2, PLANE))
     return pl.pallas_call(
         kernel,
         out_shape=(
@@ -305,7 +314,7 @@
             pltpu.VMEM((PLANE, 2) + block, BF16), pltpu.VMEM((PLANE,) + block, BF16),
             pltpu.VMEM((PLANE,) + block, BF16), pltpu.VMEM((PLANE,) + block, BF16),
             pltpu.VMEM(block, BF16), pltpu.VMEM(block, BF16),
-            many, many, many, many, many, many, eight, eight, eight, eight,
+            many, many, both, both, many, many, eight, eight, eight, eight,
             many, many, many, many, many, many, eight, eight, sem((5,)),
         ],
         compiler_params=pltpu.CompilerParams(collective_id=0, has_side_effects=True, vmem_limit_bytes=58 << 20),

time: 87.5 us -> 76.4 us (0.87)
  Pallas kernels: 83.5 us -> 72.4 us
    pallas_call x1, Pallas kernels: 83.5 us -> 72.4 us  [backward(): pl.pallas_call(kernel, out_shape=(jax.ShapeDtypeStruct((TOK, HEADS * GROU...]
where the time goes in v6:
time: 76.4 us; the launch traced here: 76.1 us
  Pallas kernels  72.4 us (95%)
  local copies, waits for them, and re-layouts  3.01 us (4%)
    pallas_call x1, Pallas kernels, backward(): pl.pallas_call(kernel, out_shape=(jax.ShapeDtypeStruct((TOK, HEADS * GROU...  72.4 us
    unnamed x7, local copies, waits for them, and re-layouts  3.01 us

profile of v6, /device:TPU:1, one launch (start us, length us, event | category | flops | bytes accessed | tf_op | source)
XLA Modules:
  0.0 76.1 jit_solution(5160244885325862723)
XLA Ops:
  0.6 72.4 %attention_backward.1 = (bf16[8,128,128]{2,1,0:T(8,128)(2,1)}, bf16[8,8,128]{2,1,0:T(8,128)(2,1)}, bf16[8,8,128]{2,1,0:T(8,128)(2,1)}) custom-call(s32[64]{0:T(128)} %order_ref.1, bf16[8,128,128]{2,1,0:T(8,128)(2,1)} %q_ref.1, bf16[8,8,128]{2,1,0:T(8,128)(2,1)} %k_ref.1, bf16[8,8,128]{2,1,0:T(8,128)(2,1)} %v_ref.1, bf16[8,128,128]{2,1,0:T(8,128)(2,1)} %g_ref.1), custom_call_target="tpu_custom_call" | custom-call | tf_op jit(solution)/shard_map/attention_backward/pallas_call | solution.py:294
  73.1 0.0 copy-start.1
  73.1 1.7 %copy.11 = bf16[8,128,128]{2,1,0:T(8,128)(2,1)} copy(bf16[8,128,128]{2,1,0:T(8,128)(2,1)} %get-tuple-element.6) | data formatting | bytes 524288
  74.8 0.0 copy-done.1
  74.8 0.0 copy-start
  74.8 0.6 copy.12
  75.4 0.1 copy-done
  75.5 0.6 copy.13
Async XLA Ops:
  73.1 1.7 %copy-start.1 = (bf16[8,8,128]{2,1,0:T(8,128)(2,1)S(1)}, bf16[8,8,128]{2,1,0:T(8,128)(2,1)}, u32[]{:S(2)}) copy-start(bf16[8,8,128]{2,1,0:T(8,128)(2,1)} %get-tuple-element.7) | copy-start | bytes 49156
  74.8 0.7 copy-start

commit v7 on v6

--- a/solution.py
+++ b/solution.py
@@ -22,12 +22,18 @@
 KEYS = CHUNKS * TOK
 SCALE = DH ** -0.5
 RATE = SCALE * math.log2(math.e)
-PAIRS = ((1, 3), (4, 12), (5, 15), (7, 13), (2, 8), (6, 14), (9, 11), (0, 10))
-UNITS = len(PAIRS)
+PART = KEYS // 2
+QUADS = ((0, 1, 3, 4), (12, 5, 15, 7), (13, 2, 8, 6), (14, 9, 11, 10))
+UNITS = 2 * len(QUADS)
+NEAR = tuple(d for quad in QUADS for d in quad if d)
 HERE = 4
 HALF = NZ // 2
+SLOTS = (slice(0, HALF), slice(HALF, NZ))
 OUTWARD = (1, 15, 2, 14, 3, 13, 4, 12, 5, 11, 6, 10, 7, 9, 8)
-NEAR = tuple(d for pair in PAIRS for d in pair if d)
+
+
+def unit(u):
+    return u // len(QUADS), QUADS[u % len(QUADS)]
 
 
 def opposite(d):
@@ -135,8 +141,8 @@
             for zz in range(NZ):
                 zs = (z + NZ + zz - HERE) % NZ
                 first = order_ref[(zs // 4) * 16 + xs * 4 + cc * 2 + ys // 2] * 64 + (ys % 2) * 32 + (zs % 4) * 8
-                at = (cc * NZ + zz) * TOK
-                pos[d, at:at + TOK, :] = first + step
+                at = (cc * HALF + zz % HALF) * TOK
+                pos[zz // HALF, d, at:at + TOK, :] = first + step
         return carry
 
     lax.fori_loop(0, PLANE, place_keys, 0)
@@ -146,14 +152,15 @@
     dqt[...] = jnp.zeros_like(dqt)
 
     kv_own.wait()
-    for part, slots in enumerate((pl.ds(0, HALF), pl.ds(HALF, HALF))):
+    for part, slots in enumerate(SLOTS):
         for d in OUTWARD:
             if (HERE - d) % NZ // HALF == part:
                 arrived(kvg.at[i, c, (HERE - d) % NZ], k_s.at[d], k_r.at[d])
         for d in NEAR:
             block = kvg.at[i, c, slots]
             start(block, block, p_s.at[part, d], p_r.at[part, d], away(d))
-    start(kvg.at[i, c], kvg.at[i, c], c_s.at[0], c_r.at[0], other)
+        block = kvg.at[i, c, slots]
+        start(block, block, c_s.at[part, 0], c_r.at[part, 0], other)
 
     lane = lax.broadcasted_iota(jnp.int32, (1, TR), 1)
 
@@ -167,22 +174,23 @@
             qt[t] = qa[2 * t:2 * t + 2].reshape(TR, DH).T
             gt[t] = ga[2 * t:2 * t + 2].reshape(TR, DH).T
 
-    def swap(d):
+    def swap(part, d):
         if d:
+            block = kvg.at[source(d), c, SLOTS[part]]
+            arrived(block, p_s.at[part, d], p_r.at[part, d])
+            start(block, block, c_s.at[part, d], c_r.at[part, d], other)
+
+    def score(u):
+        part, places = unit(u)
+        for j, d in enumerate(places):
             p = source(d)
-            for part in range(2):
-                arrived(kvg.at[p, c, pl.ds(part * HALF, HALF)], p_s.at[part, d], p_r.at[part, d])
-            start(kvg.at[p, c], kvg.at[p, c], c_s.at[d], c_r.at[d], other)
-
-    def score(u):
-        for j, d in enumerate(PAIRS[u]):
-            p = source(d)
-            arrived(kvg.at[p, 1 - c], c_s.at[d], c_r.at[d])
-            both = kvg[p].reshape(CHUNKS, 16, DH).astype(F32).reshape(CHUNKS, 2, TOK, DH)
-            k = both[:, 0].reshape(KEYS, DH).astype(BF16)
-            ks[j * KEYS:(j + 1) * KEYS, :] = k
-            kt[u, :, j * KEYS:(j + 1) * KEYS] = k.T
-            vs[j * KEYS:(j + 1) * KEYS, :] = both[:, 1].reshape(KEYS, DH).astype(BF16)
+            arrived(kvg.at[p, 1 - c, SLOTS[part]], c_s.at[part, d], c_r.at[part, d])
+            both = kvg[p, :, SLOTS[part]].reshape(2 * HALF, 16, DH).astype(F32).reshape(2 * HALF, 2, TOK, DH)
+            rows = slice(j * PART, (j + 1) * PART)
+            k = both[:, 0].reshape(PART, DH).astype(BF16)
+            ks[rows, :] = k
+            kt[u, :, rows] = k.T
+            vs[rows, :] = both[:, 1].reshape(PART, DH).astype(BF16)
 
         def tile(t, carry):
             limit = (lane // GROUP) % TOK + (y % 2) * 32
@@ -191,7 +199,7 @@
                 first = order_ref[(zs // 4) * 16 + x * 4 + c * 2 + y // 2] * 64 + (zs % 4) * 8
                 limit = limit + jnp.where(lane // DH == j, first, 0)
             s = dot(ks[...], qt[t])
-            at = jnp.concatenate((pos[PAIRS[u][0]], pos[PAIRS[u][1]]), axis=0)
+            at = jnp.concatenate([pos[part, d] for d in places], axis=0)
             s = jnp.where(jnp.concatenate((at, at), axis=1) <= limit, s, -1e30)
             old = top[t]
             new = jnp.maximum(old, jnp.max(s, axis=0, keepdims=True))
@@ -209,8 +217,8 @@
         lax.fori_loop(0, TILES, tile, 0, unroll=4)
 
     for u in range(UNITS):
-        for d in PAIRS[u]:
-            swap(d)
+        for d in unit(u)[1]:
+            swap(unit(u)[0], d)
         if u == 1:
             take_queries()
         if u >= 1:
@@ -233,19 +241,36 @@
             return carry
 
         lax.fori_loop(0, TILES, tile, 0, unroll=4)
-        for j, d in enumerate(PAIRS[u]):
-            rows = slice(j * KEYS, (j + 1) * KEYS)
-            both = jnp.stack(((dk[rows, :] * SCALE).reshape(CHUNKS, TOK, DH), dv[rows, :].reshape(CHUNKS, TOK, DH)), axis=1)
-            dkv[d] = both.reshape(2, NZ, 16, DH).astype(BF16)
-            start(dkv.at[d, 1 - c], cx.at[d], d_s.at[d], d_r.at[d], other)
+        part, places = unit(u)
+        for j, d in enumerate(places):
+            rows = slice(j * PART, (j + 1) * PART)
+            both = jnp.stack(
+                ((dk[rows, :] * SCALE).reshape(2 * HALF, TOK, DH), dv[rows, :].reshape(2 * HALF, TOK, DH)), axis=1
+            )
+            dkv[d, :, SLOTS[part]] = both.reshape(2, HALF, 16, DH).astype(BF16)
+            start(dkv.at[d, 1 - c, SLOTS[part]], cx.at[d, SLOTS[part]], d_s.at[part, d], d_r.at[part, d], other)
 
     def along(u):
-        for d in PAIRS[u]:
-            arrived(cx.at[d], d_s.at[d], d_r.at[d])
+        part, places = unit(u)
+        slots = SLOTS[part]
+        for d in places:
+            arrived(cx.at[d, slots], d_s.at[part, d], d_r.at[part, d])
             if d:
                 back = opposite(d)
-                pst[d] = (dkv[d, c].astype(F32) + cx[d].astype(F32)).astype(BF16)
-                start(pst.at[d], pr.at[back], e_s.at[back], e_r.at[back], away(back))
+                pst[d, slots] = (dkv[d, c, slots].astype(F32) + cx[d, slots].astype(F32)).astype(BF16)
+                start(pst.at[d, slots], pr.at[back, slots], e_s.at[part, back], e_r.at[part, back], away(back))
+
+    def finish(part):
+        slots = SLOTS[part]
+        here = dkv[0, c, slots].astype(F32) + cx[0, slots].astype(F32)
+        for d in reversed(NEAR):
+            arrived(pr.at[d, slots], e_s.at[part, d], e_r.at[part, d])
+            here = here + pr[d, slots].astype(F32)
+        fst[slots] = here.astype(BF16)
+        for d in reversed(OUTWARD):
+            at = (HERE + d) % NZ
+            if at // HALF == part:
+                start(fst.at[at], fin.at[z], f_s.at[d], f_r.at[d], device(x, y, (z + d) % NZ, c))
 
     late = tuple(reversed(range(UNITS)))
     for k, u in enumerate(late):
@@ -253,21 +278,14 @@
         if k:
             along(late[k - 1])
     along(late[-1])
+    finish(1)
     for t in range(TILES):
         dqs[2 * t:2 * t + 2] = (dqt[t] * SCALE).T.astype(BF16).reshape(2, TOK, GROUP, DH)
     rows = pl.ds(head * GROUP, GROUP)
     dq_own = local(dqs.at[0], dqh_ref.at[:, rows, :], 2)
     for o in range(1, HEADS):
         start(dqs.at[o], dqh_ref.at[:, rows, :], o_s.at[o], o_r.at[o], device(x, y, got_from(o, z), c))
-    part = dkv[0, c].astype(F32) + cx[0].astype(F32)
-    for u in late:
-        for d in PAIRS[u]:
-            if d:
-                arrived(pr.at[d], e_s.at[d], e_r.at[d])
-                part = part + pr[d].astype(F32)
-    fst[...] = part.astype(BF16)
-    for d in reversed(OUTWARD):
-        start(fst.at[(HERE + d) % NZ], fin.at[z], f_s.at[d], f_r.at[d], device(x, y, (z + d) % NZ, c))
+    finish(0)
     kv_home = local(fst.at[HERE], fin.at[z], 4)
     kv_home.wait()
     for d in range(1, NZ):
@@ -306,7 +324,7 @@
             pltpu.VMEM((TILES, DH, TR), BF16), pltpu.VMEM((TILES, DH, TR), BF16),
             pltpu.VMEM((PLANE, 2) + block, BF16),
             pltpu.VMEM((2 * KEYS, DH), BF16), pltpu.VMEM((2 * KEYS, DH), BF16), pltpu.VMEM((UNITS, DH, 2 * KEYS), BF16),
-            pltpu.VMEM((PLANE, KEYS, DH), jnp.int32),
+            pltpu.VMEM((2, PLANE, PART, DH), jnp.int32),
             pltpu.VMEM((UNITS, TILES, 2 * KEYS, TR), F32), pltpu.VMEM((UNITS, TILES, 2 * KEYS, TR), F32),
             pltpu.VMEM((UNITS, TILES, 1, TR), F32), stat, stat, stat,
             pltpu.VMEM((2 * KEYS, DH), F32), pltpu.VMEM((2 * KEYS, DH), F32),
@@ -314,8 +332,8 @@
             pltpu.VMEM((PLANE, 2) + block, BF16), pltpu.VMEM((PLANE,) + block, BF16),
             pltpu.VMEM((PLANE,) + block, BF16), pltpu.VMEM((PLANE,) + block, BF16),
             pltpu.VMEM(block, BF16), pltpu.VMEM(block, BF16),
-            many, many, both, both, many, many, eight, eight, eight, eight,
-            many, many, many, many, many, many, eight, eight, sem((5,)),
+            many, many, both, both, both, both, eight, eight, eight, eight,
+            both, both, both, both, many, many, eight, eight, sem((5,)),
         ],
         compiler_params=pltpu.CompilerParams(collective_id=0, has_side_effects=True, vmem_limit_bytes=58 << 20),
         name="attention_backward",

time: 76.4 us -> 76.6 us (level)
  no operation moved by 1% of the time
where the time goes in v7:
time: 76.6 us; the launch traced here: 76.4 us
  Pallas kernels  72.7 us (95%)
  local copies, waits for them, and re-layouts  3.01 us (4%)
    pallas_call x1, Pallas kernels, backward(): pl.pallas_call(kernel, out_shape=(jax.ShapeDtypeStruct((TOK, HEADS * GROU...  72.7 us
    unnamed x7, local copies, waits for them, and re-layouts  3.01 us

profile of v7, /device:TPU:1, one launch (start us, length us, event | category | flops | bytes accessed | tf_op | source)
XLA Modules:
  0.0 76.4 jit_solution(3202667277636511304)
XLA Ops:
  0.6 72.7 %attention_backward.1 = (bf16[8,128,128]{2,1,0:T(8,128)(2,1)}, bf16[8,8,128]{2,1,0:T(8,128)(2,1)}, bf16[8,8,128]{2,1,0:T(8,128)(2,1)}) custom-call(s32[64]{0:T(128)} %order_ref.1, bf16[8,128,128]{2,1,0:T(8,128)(2,1)} %q_ref.1, bf16[8,8,128]{2,1,0:T(8,128)(2,1)} %k_ref.1, bf16[8,8,128]{2,1,0:T(8,128)(2,1)} %v_ref.1, bf16[8,128,128]{2,1,0:T(8,128)(2,1)} %g_ref.1), custom_call_target="tpu_custom_call" | custom-call | tf_op jit(solution)/shard_map/attention_backward/pallas_call | solution.py:312
  73.3 0.0 copy-start.1
  73.3 1.7 %copy.11 = bf16[8,128,128]{2,1,0:T(8,128)(2,1)} copy(bf16[8,128,128]{2,1,0:T(8,128)(2,1)} %get-tuple-element.6) | data formatting | bytes 524288
  75.0 0.0 copy-done.1
  75.0 0.0 copy-start
  75.0 0.6 copy.12
  75.6 0.1 copy-done
  75.7 0.6 copy.13
Async XLA Ops:
  73.3 1.7 %copy-start.1 = (bf16[8,8,128]{2,1,0:T(8,128)(2,1)S(1)}, bf16[8,8,128]{2,1,0:T(8,128)(2,1)}, u32[]{:S(2)}) copy-start(bf16[8,8,128]{2,1,0:T(8,128)(2,1)} %get-tuple-element.7) | copy-start | bytes 49156
  75.0 0.7 copy-start
